TPU v7x, 32 devices: a whole 2x2x4 slice. The times are simulated.
32 devices in a mesh: head: 4 (over y, x), qblk: 8 (over z, core).
Axes of the slice: x: 2, y: 2, z: 4, core: 2. Of those that a mesh axis runs over, the one named last changes fastest.
Arguments:
- queries: bfloat16 [16384, 4096], P(('qblk', 'head')), may hold values from -6 to 6
- key_states: bfloat16 [16384, 1024], P(('qblk', 'head')), may hold values from -6 to 6
- value_states: bfloat16 [16384, 1024], P(('qblk', 'head')), may hold values from -6 to 6
- vertical_blocks: int32 [32, 5], replicated, may hold values from 0 to 254, as said below
- slash_offsets: int32 [32, 8], replicated, may hold values from 1 to 64, as said below
Outputs:
- attended: bfloat16 [16384, 4096], P(('qblk', 'head'))
Inputs may be any that keep to these rules, and one draw needn't show every extreme that they name: `vertical_blocks`: each head names 5 distinct blocks, among them block 0 and block 254. `slash_offsets`: each head names 8 distinct offsets, among them 1 and 64.
All inputs are finite; a program needn't handle non-finite values.
Results may differ from a plain program's by a relative error of at most 0.0033.
Values may be sent and summed in bfloat16 or wider, within the bound.
A program may use at most 64 MiB of HBM per device.

v0:
```python
import jax
import jax.numpy as jnp
from jax import lax
from jax.sharding import PartitionSpec as P

H = 32
KVH = 8
HD = 128
BLK = 64


def from_behind(value, axis, steps):
    count = lax.axis_size(axis)
    leading, last = (max(0, -steps), min(count, count - steps))
    return lax.ppermute(value, axis, [(source, source + steps) for source in range(leading, last)])


def attend_group(
    query_block_list,
    diagonal_key_block,
    diagonal_value_block,
    slash_key_block,
    slash_value_block,
    vertical_key_block,
    vertical_value_block,
    block_ids,
    slash_row,
    vert_row,
):
    number_format = jnp.float32
    logit_scale = query_block_list.shape[-1] ** (-0.5)
    diagonal_scores = (
        jnp.einsum(
            "pwr,pgr->pwg",
            query_block_list,
            diagonal_key_block,
            preferred_element_type=number_format,
        )
        * logit_scale
    )
    slash_scores = (
        jnp.einsum(
            "pzf,opwf->pzow",
            query_block_list,
            slash_key_block,
            preferred_element_type=number_format,
        )
        * logit_scale
    )
    vertical_scores = (
        jnp.einsum(
            "ihx,zsx->ihzs",
            query_block_list,
            vertical_key_block,
            preferred_element_type=number_format,
        )
        * logit_scale
    )
    block_len = query_block_list.shape[1]
    causal = jnp.arange(block_len)[:, None] >= jnp.arange(block_len)[None, :]
    diagonal_scores = jnp.where(causal[None], diagonal_scores, -jnp.inf)
    slash_ok = block_ids[:, None] - slash_row[None, :] >= 0
    slash_scores = jnp.where(slash_ok[:, None, :, None], slash_scores, -jnp.inf)
    block_gap = block_ids[:, None] - vert_row[None, :]
    slash_hit = jnp.any(block_gap[:, :, None] == slash_row[None, None, :], axis=2)
    vert_ok = (block_gap > 0) & jnp.logical_not(slash_hit)
    vertical_scores = jnp.where(vert_ok[:, None, :, None], vertical_scores, -jnp.inf)
    row_max = jnp.maximum(
        jnp.max(diagonal_scores, axis=2),
        jnp.maximum(jnp.max(slash_scores, axis=(2, 3)), jnp.max(vertical_scores, axis=(2, 3))),
    )
    diagonal_weights = jnp.exp(diagonal_scores - row_max[:, :, None])
    slash_weights = jnp.exp(slash_scores - row_max[:, :, None, None])
    vertical_weights = jnp.exp(vertical_scores - row_max[:, :, None, None])
    row_total = (
        jnp.sum(diagonal_weights, axis=2)
        + jnp.sum(slash_weights, axis=(2, 3))
        + jnp.sum(vertical_weights, axis=(2, 3))
    )
    weight_total = jnp.einsum(
        "rmt,rtl->rml",
        diagonal_weights.astype(jnp.bfloat16),
        diagonal_value_block,
        preferred_element_type=number_format,
    )
    weight_total = weight_total + jnp.einsum(
        "mnop,ompj->mnj",
        slash_weights.astype(jnp.bfloat16),
        slash_value_block,
        preferred_element_type=number_format,
    )
    weight_total = weight_total + jnp.einsum(
        "tiyx,yxf->tif",
        vertical_weights.astype(jnp.bfloat16),
        vertical_value_block,
        preferred_element_type=number_format,
    )
    return (weight_total / row_total[:, :, None]).astype(jnp.bfloat16)


def take_vertical(piece_rows, start_row, wanted, kv_select, current):
    count = piece_rows.shape[1]
    offset = wanted - start_row
    inside = (offset >= 0) & (offset < count)
    picked = piece_rows[:, jnp.clip(offset, 0, count - 1), kv_select[:, None]]
    return jnp.where(inside[None, :, :, None], picked, current)


def per_device(queries, key_states, value_states, vertical_blocks, slash_offsets):
    head_count = lax.axis_size("head")
    head_index = lax.axis_index("head")
    block_index = lax.axis_index("qblk")
    rows_in = queries.shape[0]
    q_heads = H // head_count
    copies = max(1, head_count // KVH)
    kv_heads = KVH * copies // head_count
    q_split = queries.reshape(1, rows_in, H, HD)
    kv_pair = jnp.stack([key_states, value_states], axis=0).reshape(2, rows_in, KVH, HD)
    if copies > 1:
        kv_pair = jnp.repeat(kv_pair, copies, axis=2)
    q_local, kv_local = (
        lax.all_to_all(q_split, "head", split_axis=2, concat_axis=1, tiled=True),
        lax.all_to_all(kv_pair, "head", split_axis=2, concat_axis=1, tiled=True),
    )
    row_count = kv_local.shape[1]
    first_row = block_index * row_count
    vert_mine = lax.dynamic_slice_in_dim(vertical_blocks, head_index * q_heads, q_heads, 0)
    slash_mine = lax.dynamic_slice_in_dim(slash_offsets, head_index * q_heads, q_heads, 0)
    vert_count = vert_mine.shape[1]
    slash_count = slash_mine.shape[1]
    kv_select = jnp.arange(q_heads, dtype=jnp.int32) // (q_heads // kv_heads)
    want_vert = (
        vert_mine[:, :, None] * BLK + jnp.arange(BLK, dtype=jnp.int32)[None, None, :]
    ).reshape(q_heads, vert_count * BLK)
    empty_vert = jnp.zeros((2, q_heads, vert_count * BLK, HD), jnp.bfloat16)
    two_back = from_behind(kv_local, "qblk", 2)
    one_back = from_behind(kv_local, "qblk", 1)
    window = jnp.concatenate([two_back, one_back, kv_local], axis=1)
    own_term = take_vertical(kv_local, first_row, want_vert, kv_select, empty_vert)
    vert_rows = lax.psum(own_term, "qblk").astype(jnp.float32).astype(jnp.bfloat16)
    group_rows = min(512, row_count)
    group_blocks = group_rows // BLK
    front = 2 * row_count
    head_outputs = []
    for head_slot in range(q_heads):
        kv_slot = head_slot // (q_heads // kv_heads)
        k_window = window[0, :, kv_slot]
        v_window = window[1, :, kv_slot]
        q_head = q_local[0, :, head_slot]
        vertical_key_block = vert_rows[0, head_slot].reshape(vert_count, BLK, HD)
        vertical_value_block = vert_rows[1, head_slot].reshape(vert_count, BLK, HD)
        slash_row = slash_mine[head_slot]
        vert_row = vert_mine[head_slot]

        def one_group(group_index):
            start_row = group_index * group_rows
            query_block_list = lax.dynamic_slice_in_dim(q_head, start_row, group_rows, 0).reshape(
                group_blocks, BLK, HD
            )
            diagonal_key_block = lax.dynamic_slice_in_dim(
                k_window, front + start_row, group_rows, 0
            ).reshape(group_blocks, BLK, HD)
            diagonal_value_block = lax.dynamic_slice_in_dim(
                v_window, front + start_row, group_rows, 0
            ).reshape(group_blocks, BLK, HD)

            def slash_rows(source, offset_blocks):
                return lax.dynamic_slice_in_dim(
                    source, front + start_row - offset_blocks * BLK, group_rows, 0
                )

            slash_key_block = jax.vmap(slash_rows, in_axes=(None, 0))(k_window, slash_row).reshape(
                slash_count, group_blocks, BLK, HD
            )
            slash_value_block = jax.vmap(slash_rows, in_axes=(None, 0))(
                v_window, slash_row
            ).reshape(slash_count, group_blocks, BLK, HD)
            block_ids = (
                block_index * (row_count // BLK)
                + start_row // BLK
                + jnp.arange(group_blocks, dtype=jnp.int32)
            )
            return attend_group(
                query_block_list,
                diagonal_key_block,
                diagonal_value_block,
                slash_key_block,
                slash_value_block,
                vertical_key_block,
                vertical_value_block,
                block_ids,
                slash_row,
                vert_row,
            )

        grouped = lax.map(one_group, jnp.arange(row_count // group_rows, dtype=jnp.int32))
        head_outputs.append(grouped.reshape(row_count, HD))
    stacked = jnp.stack(head_outputs, axis=1)
    returned = lax.all_to_all(stacked, "head", split_axis=0, concat_axis=1, tiled=True)
    return returned.reshape(returned.shape[0], H * HD)


def solution(mesh):
    return jax.shard_map(
        per_device,
        mesh=mesh,
        in_specs=(
            P(("qblk", "head"), None),
            P(("qblk", "head"), None),
            P(("qblk", "head"), None),
            P(),
            P(),
        ),
        out_specs=P(("qblk", "head"), None),
        check_vma=False,
    )
```

profile of v0, /device:TPU:24, one launch (start us, length us, event | category | flops | bytes accessed | tf_op | source)
XLA Modules:
  0.0 1843.2 jit_solution(8740114369293502436)
XLA Ops:
  73.1 61.0 %all-reduce.10.cloned.1.call-done = bf16[2,8,320,128]{3,2,1,0:T(8,128)(2,1)} async-done(((bf16[2,8,320,128]{3,2,1,0:T(8,128)(2,1)}), bf16[2,8,320,128]{3,2,1,0:T(8,128)(2,1)}) %all-reduce.10.cloned.1.call-update) | async-done | bytes 1310736 | tf_op jit(solution)/shard_map/psum | solution.py:140
  165.7 28.1 %pad_maximum_fusion = bf16[2,6144,2,128]{3,0,2,1:T(2,128)(2,1)S(1)} fusion(bf16[2,2048,2,128]{3,0,2,1:T(2,128)(2,1)S(1)} %bitcast.854, bf16[2,2048,2,128]{3,0,2,1:T(2,128)(2,1)} %collective-permute-done.1, bf16[2,2048,2,128]{3,0,2,1:T(2,128)(2,1)} %collective-permute-done), kind=kLoop, calls=%fused_computation.417 | loop fusion | flops 6291456 | bytes 12582912 | tf_op jit(solution)/shard_map/concatenate | solution.py:138
  206.3 193.5 %while.133 = (s32[]{:T(128)}, bf16[4,8,64,128]{3,2,1,0:T(8,128)(2,1)}, s32[4]{0:T(128)S(1)}, bf16[2048,128]{1,0:T(8,128)(2,1)}, bf16[6144,128]{1,0:T(8,128)(2,1)...) while((s32[]{:T(128)}, ...), condition=%wide.region_18.19_spmd, body=%wide.region_10.18_spmd.sunk | while | flops 239407072 | bytes 13391324 | solution.py:196
  208.7 18.7 %while.154 = (s32[]{:T(128)}, bf16[6144,128]{1,0:T(8,128)(2,1)}, s32[8,2]{0,1:T(2,128)S(1)}, bf16[8,512,128]{2,1,0:T(8,128)(2,1)S(1)}, s32[]{:T(128)}) while((s32[]{:T(128)}, bf16[6144,128]{1,0:T(8,128)(2,1)}, s32[8,2]{0,1:T(2,128)S(1)}, bf16[8,512,128]{2,1,0:T(8,128)(2,1)S(1)}, s32[]{:T(128)}) %tuple.590), condition=%wide.while_cond.2, body=%wide.while_body.2.sunk | while | flops 2 | bytes 262241 | solution.py:168
  257.1 18.7 %while.154 = (s32[]{:T(128)}, bf16[6144,128]{1,0:T(8,128)(2,1)}, s32[8,2]{0,1:T(2,128)S(1)}, bf16[8,512,128]{2,1,0:T(8,128)(2,1)S(1)}, s32[]{:T(128)}) while((s32[]{:T(128)}, bf16[6144,128]{1,0:T(8,128)(2,1)}, s32[8,2]{0,1:T(2,128)S(1)}, bf16[8,512,128]{2,1,0:T(8,128)(2,1)S(1)}, s32[]{:T(128)}) %tuple.590), condition=%wide.while_cond.2, body=%wide.while_body.2.sunk | while | flops 2 | bytes 262241 | solution.py:168
  305.5 18.7 %while.154 = (s32[]{:T(128)}, bf16[6144,128]{1,0:T(8,128)(2,1)}, s32[8,2]{0,1:T(2,128)S(1)}, bf16[8,512,128]{2,1,0:T(8,128)(2,1)S(1)}, s32[]{:T(128)}) while((s32[]{:T(128)}, bf16[6144,128]{1,0:T(8,128)(2,1)}, s32[8,2]{0,1:T(2,128)S(1)}, bf16[8,512,128]{2,1,0:T(8,128)(2,1)S(1)}, s32[]{:T(128)}) %tuple.590), condition=%wide.while_cond.2, body=%wide.while_body.2.sunk | while | flops 2 | bytes 262241 | solution.py:168
  353.9 18.7 %while.154 = (s32[]{:T(128)}, bf16[6144,128]{1,0:T(8,128)(2,1)}, s32[8,2]{0,1:T(2,128)S(1)}, bf16[8,512,128]{2,1,0:T(8,128)(2,1)S(1)}, s32[]{:T(128)}) while((s32[]{:T(128)}, bf16[6144,128]{1,0:T(8,128)(2,1)}, s32[8,2]{0,1:T(2,128)S(1)}, bf16[8,512,128]{2,1,0:T(8,128)(2,1)S(1)}, s32[]{:T(128)}) %tuple.590), condition=%wide.while_cond.2, body=%wide.while_body.2.sunk | while | flops 2 | bytes 262241 | solution.py:168
  400.7 188.7 %while.130 = (s32[]{:T(128)}, bf16[4,8,64,128]{3,2,1,0:T(8,128)(2,1)}, s32[4]{0:T(128)S(1)}, bf16[2048,128]{1,0:T(8,128)(2,1)}, bf16[6144,128]{1,0:T(8,128)(2,1)...) while((s32[]{:T(128)}, ...), condition=%wide.region_9.10_spmd, body=%wide.region_1.9_spmd.sunk | while | flops 239407072 | bytes 13719032 | solution.py:196
  403.3 17.8 while.152
  450.5 17.8 while.152
  497.6 17.8 while.152
  544.7 17.8 while.152
  570.1 15.4 while.153
  592.2 195.3 %while.136 = (s32[]{:T(128)}, bf16[4,8,64,128]{3,2,1,0:T(8,128)(2,1)}, s32[4]{0:T(128)S(1)}, bf16[2048,128]{1,0:T(8,128)(2,1)}, bf16[6144,128]{1,0:T(8,128)(2,1)...) while((s32[]{:T(128)}, ...), condition=%wide.region_27.28_spmd, body=%wide.region_19.27_spmd.sunk | while | flops 239407072 | bytes 13719032 | solution.py:196
  594.8 18.5 %while.156 = (s32[]{:T(128)}, bf16[6144,128]{1,0:T(8,128)(2,1)}, s32[8,2]{0,1:T(2,128)S(1)}, bf16[8,512,128]{2,1,0:T(8,128)(2,1)S(1)}, s32[]{:T(128)}) while((s32[]{:T(128)}, bf16[6144,128]{1,0:T(8,128)(2,1)}, s32[8,2]{0,1:T(2,128)S(1)}, bf16[8,512,128]{2,1,0:T(8,128)(2,1)S(1)}, s32[]{:T(128)}) %tuple.584), condition=%wide.while_cond.4, body=%wide.while_body.4.sunk | while | flops 2 | bytes 262241 | solution.py:168
  620.9 16.2 while.157
  643.6 18.5 %while.156 = (s32[]{:T(128)}, bf16[6144,128]{1,0:T(8,128)(2,1)}, s32[8,2]{0,1:T(2,128)S(1)}, bf16[8,512,128]{2,1,0:T(8,128)(2,1)S(1)}, s32[]{:T(128)}) while((s32[]{:T(128)}, bf16[6144,128]{1,0:T(8,128)(2,1)}, s32[8,2]{0,1:T(2,128)S(1)}, bf16[8,512,128]{2,1,0:T(8,128)(2,1)S(1)}, s32[]{:T(128)}) %tuple.584), condition=%wide.while_cond.4, body=%wide.while_body.4.sunk | while | flops 2 | bytes 262241 | solution.py:168
  669.7 16.2 while.157
  692.5 18.5 %while.156 = (s32[]{:T(128)}, bf16[6144,128]{1,0:T(8,128)(2,1)}, s32[8,2]{0,1:T(2,128)S(1)}, bf16[8,512,128]{2,1,0:T(8,128)(2,1)S(1)}, s32[]{:T(128)}) while((s32[]{:T(128)}, bf16[6144,128]{1,0:T(8,128)(2,1)}, s32[8,2]{0,1:T(2,128)S(1)}, bf16[8,512,128]{2,1,0:T(8,128)(2,1)S(1)}, s32[]{:T(128)}) %tuple.584), condition=%wide.while_cond.4, body=%wide.while_body.4.sunk | while | flops 2 | bytes 262241 | solution.py:168
  718.5 16.2 while.157
  741.3 18.5 %while.156 = (s32[]{:T(128)}, bf16[6144,128]{1,0:T(8,128)(2,1)}, s32[8,2]{0,1:T(2,128)S(1)}, bf16[8,512,128]{2,1,0:T(8,128)(2,1)S(1)}, s32[]{:T(128)}) while((s32[]{:T(128)}, bf16[6144,128]{1,0:T(8,128)(2,1)}, s32[8,2]{0,1:T(2,128)S(1)}, bf16[8,512,128]{2,1,0:T(8,128)(2,1)S(1)}, s32[]{:T(128)}) %tuple.584), condition=%wide.while_cond.4, body=%wide.while_body.4.sunk | while | flops 2 | bytes 262241 | solution.py:168
  767.3 16.2 while.157
  788.5 190.9 %while.139 = (s32[]{:T(128)}, bf16[4,8,64,128]{3,2,1,0:T(8,128)(2,1)}, s32[4]{0:T(128)S(1)}, bf16[2048,128]{1,0:T(8,128)(2,1)}, bf16[6144,128]{1,0:T(8,128)(2,1)...) while((s32[]{:T(128)}, ...), condition=%wide.region_36.37_spmd, body=%wide.region_28.36_spmd.sunk | while | flops 239407072 | bytes 13391324 | solution.py:196
  790.8 18.1 while.158
  816.4 15.8 while.159
  838.5 18.1 while.158
  864.1 15.8 while.159
  886.1 18.1 while.158
  911.8 15.8 while.159
  933.8 18.1 while.158
  959.4 15.8 while.159
  984.8 191.6 %while.142 = (s32[]{:T(128)}, bf16[4,8,64,128]{3,2,1,0:T(8,128)(2,1)}, s32[4]{0:T(128)S(1)}, bf16[2048,128]{1,0:T(8,128)(2,1)}, bf16[6144,128]{1,0:T(8,128)(2,1)...) while((s32[]{:T(128)}, ...), condition=%wide.region_45.46_spmd, body=%wide.region_37.45_spmd.sunk | while | flops 239407072 | bytes 13391324 | solution.py:196
  987.2 17.7 while.160
  1035.1 17.7 while.160
  1083.0 17.7 while.160
  1130.9 17.7 while.160
  1177.3 195.9 %while.145 = (s32[]{:T(128)}, bf16[4,8,64,128]{3,2,1,0:T(8,128)(2,1)}, s32[4]{0:T(128)S(1)}, bf16[2048,128]{1,0:T(8,128)(2,1)}, bf16[6144,128]{1,0:T(8,128)(2,1)...) while((s32[]{:T(128)}, ...), condition=%wide.region_54.55_spmd, body=%wide.region_46.54_spmd.sunk | while | flops 239407072 | bytes 13391324 | solution.py:196
  1179.7 18.7 %while.162 = (s32[]{:T(128)}, bf16[6144,128]{1,0:T(8,128)(2,1)}, s32[8,2]{0,1:T(2,128)S(1)}, bf16[8,512,128]{2,1,0:T(8,128)(2,1)S(1)}, s32[]{:T(128)}) while((s32[]{:T(128)}, bf16[6144,128]{1,0:T(8,128)(2,1)}, s32[8,2]{0,1:T(2,128)S(1)}, bf16[8,512,128]{2,1,0:T(8,128)(2,1)S(1)}, s32[]{:T(128)}) %tuple.566), condition=%wide.while_cond.10, body=%wide.while_body.10.sunk | while | flops 2 | bytes 262241 | solution.py:168
  1205.9 16.4 while.163
  1228.7 18.7 %while.162 = (s32[]{:T(128)}, bf16[6144,128]{1,0:T(8,128)(2,1)}, s32[8,2]{0,1:T(2,128)S(1)}, bf16[8,512,128]{2,1,0:T(8,128)(2,1)S(1)}, s32[]{:T(128)}) while((s32[]{:T(128)}, bf16[6144,128]{1,0:T(8,128)(2,1)}, s32[8,2]{0,1:T(2,128)S(1)}, bf16[8,512,128]{2,1,0:T(8,128)(2,1)S(1)}, s32[]{:T(128)}) %tuple.566), condition=%wide.while_cond.10, body=%wide.while_body.10.sunk | while | flops 2 | bytes 262241 | solution.py:168
  1254.9 16.4 while.163
  1277.6 18.7 %while.162 = (s32[]{:T(128)}, bf16[6144,128]{1,0:T(8,128)(2,1)}, s32[8,2]{0,1:T(2,128)S(1)}, bf16[8,512,128]{2,1,0:T(8,128)(2,1)S(1)}, s32[]{:T(128)}) while((s32[]{:T(128)}, bf16[6144,128]{1,0:T(8,128)(2,1)}, s32[8,2]{0,1:T(2,128)S(1)}, bf16[8,512,128]{2,1,0:T(8,128)(2,1)S(1)}, s32[]{:T(128)}) %tuple.566), condition=%wide.while_cond.10, body=%wide.while_body.10.sunk | while | flops 2 | bytes 262241 | solution.py:168
  1303.9 16.4 while.163
  1326.6 18.7 %while.162 = (s32[]{:T(128)}, bf16[6144,128]{1,0:T(8,128)(2,1)}, s32[8,2]{0,1:T(2,128)S(1)}, bf16[8,512,128]{2,1,0:T(8,128)(2,1)S(1)}, s32[]{:T(128)}) while((s32[]{:T(128)}, bf16[6144,128]{1,0:T(8,128)(2,1)}, s32[8,2]{0,1:T(2,128)S(1)}, bf16[8,512,128]{2,1,0:T(8,128)(2,1)S(1)}, s32[]{:T(128)}) %tuple.566), condition=%wide.while_cond.10, body=%wide.while_body.10.sunk | while | flops 2 | bytes 262241 | solution.py:168
  1352.8 16.4 while.163
  1374.1 196.3 %while.148 = (s32[]{:T(128)}, bf16[4,8,64,128]{3,2,1,0:T(8,128)(2,1)}, s32[4]{0:T(128)S(1)}, bf16[2048,128]{1,0:T(8,128)(2,1)}, bf16[6144,128]{1,0:T(8,128)(2,1)...) while((s32[]{:T(128)}, ...), condition=%wide.region_63.64_spmd, body=%wide.region_55.63_spmd.sunk | while | flops 239407072 | bytes 13719032 | solution.py:196
  1376.8 18.7 %while.164 = (s32[]{:T(128)}, bf16[6144,128]{1,0:T(8,128)(2,1)}, s32[8,2]{0,1:T(2,128)S(1)}, bf16[8,512,128]{2,1,0:T(8,128)(2,1)S(1)}, s32[]{:T(128)}) while((s32[]{:T(128)}, bf16[6144,128]{1,0:T(8,128)(2,1)}, s32[8,2]{0,1:T(2,128)S(1)}, bf16[8,512,128]{2,1,0:T(8,128)(2,1)S(1)}, s32[]{:T(128)}) %tuple.560), condition=%wide.while_cond.12, body=%wide.while_body.12.sunk | while | flops 2 | bytes 262241 | solution.py:168
  1403.0 16.4 while.165
  1425.8 18.7 %while.164 = (s32[]{:T(128)}, bf16[6144,128]{1,0:T(8,128)(2,1)}, s32[8,2]{0,1:T(2,128)S(1)}, bf16[8,512,128]{2,1,0:T(8,128)(2,1)S(1)}, s32[]{:T(128)}) while((s32[]{:T(128)}, bf16[6144,128]{1,0:T(8,128)(2,1)}, s32[8,2]{0,1:T(2,128)S(1)}, bf16[8,512,128]{2,1,0:T(8,128)(2,1)S(1)}, s32[]{:T(128)}) %tuple.560), condition=%wide.while_cond.12, body=%wide.while_body.12.sunk | while | flops 2 | bytes 262241 | solution.py:168
  1452.0 16.4 while.165
  1474.9 18.7 %while.164 = (s32[]{:T(128)}, bf16[6144,128]{1,0:T(8,128)(2,1)}, s32[8,2]{0,1:T(2,128)S(1)}, bf16[8,512,128]{2,1,0:T(8,128)(2,1)S(1)}, s32[]{:T(128)}) while((s32[]{:T(128)}, bf16[6144,128]{1,0:T(8,128)(2,1)}, s32[8,2]{0,1:T(2,128)S(1)}, bf16[8,512,128]{2,1,0:T(8,128)(2,1)S(1)}, s32[]{:T(128)}) %tuple.560), condition=%wide.while_cond.12, body=%wide.while_body.12.sunk | while | flops 2 | bytes 262241 | solution.py:168
  1501.1 16.4 while.165
  1523.9 18.7 %while.164 = (s32[]{:T(128)}, bf16[6144,128]{1,0:T(8,128)(2,1)}, s32[8,2]{0,1:T(2,128)S(1)}, bf16[8,512,128]{2,1,0:T(8,128)(2,1)S(1)}, s32[]{:T(128)}) while((s32[]{:T(128)}, bf16[6144,128]{1,0:T(8,128)(2,1)}, s32[8,2]{0,1:T(2,128)S(1)}, bf16[8,512,128]{2,1,0:T(8,128)(2,1)S(1)}, s32[]{:T(128)}) %tuple.560), condition=%wide.while_cond.12, body=%wide.while_body.12.sunk | while | flops 2 | bytes 262241 | solution.py:168
  1550.1 16.4 while.165
  1571.4 191.2 %while.151 = (s32[]{:T(128)}, bf16[4,8,64,128]{3,2,1,0:T(8,128)(2,1)}, s32[4]{0:T(128)S(1)}, bf16[2048,128]{1,0:T(8,128)(2,1)}, bf16[6144,128]{1,0:T(8,128)(2,1)...) while((s32[]{:T(128)}, ...), condition=%wide.region_72.73_spmd, body=%wide.region_64.72_spmd.sunk | while | flops 239407072 | bytes 13391324 | solution.py:196
  1573.8 18.2 while.166
  1599.4 15.8 while.167
  1621.5 18.2 while.166
  1647.2 15.8 while.167
  1669.3 18.2 while.166
  1695.0 15.8 while.167
  1717.1 18.2 while.166
  1742.8 15.8 while.167
  1780.5 41.5 %all_to_all.51 = bf16[2048,8,128]{2,1,0:T(8,128)(2,1)} all-to-all(bf16[2048,8,128]{2,1,0:T(8,128)(2,1)S(1)} %copy.361), channel_id=1, replica_groups=mesh['head'=4,'qblk'=8] {'head'}, dimensions={0} | all-to-all | bytes 8388608 | tf_op jit(solution)/shard_map/all_to_all | solution.py:199
  (2543 shorter events, 1835.0 us)
Async XLA Ops:
  6.5 59.8 %copy-start = (s32[32,8]{0,1:T(8,128)S(1)}, s32[32,8]{0,1:T(8,128)}, u32[]{:S(2)}) copy-start(s32[32,8]{0,1:T(8,128)} %param.25) | copy-start | bytes 3076
  11.3 29.7 %all-to-all-start.1 = ((bf16[2,512,8,128]{1,3,0,2:T(8,128)(2,1)}), bf16[2,512,8,128]{1,3,0,2:T(8,128)(2,1)}, u32[]{:S(2)}, u32[]{:S(2)}) async-start(bf16[2,512,8,128]{1,3,0,2:T(8,128)(2,1)} %copy.355), calls=%async_computation.1 | async-start | bytes 4194304 | tf_op jit(solution)/shard_map/all_to_all | solution.py:123
  28.6 17.3 copy-start.24
  41.0 95.5 %all-to-all-start = ((bf16[1,512,32,128]{3,1,0,2:T(8,128)(2,1)}), bf16[1,512,32,128]{3,1,0,2:T(8,128)(2,1)}, u32[]{:S(2)}, u32[]{:S(2)}) async-start(bf16[1,512,32,128]{3,1,0,2:T(8,128)(2,1)} %copy.350), calls=%async_computation | async-start | bytes 8388608 | tf_op jit(solution)/shard_map/all_to_all | solution.py:122
  45.9 88.2 %all-reduce.10.cloned.1.call-start = ((), (), s32[]{:S(2)}) async-start(), calls=%async_computation.3 | async-start | bytes 2621440 | tf_op jit(solution)/shard_map/psum | solution.py:140
  69.9 84.9 %collective-permute-start = (bf16[2,2048,2,128]{3,0,2,1:T(2,128)(2,1)}, bf16[2,2048,2,128]{3,0,2,1:T(2,128)(2,1)}, u32[]{:S(2)}, u32[]{:S(2)}) collective-permute-start(bf16[2,2048,2,128]{3,0,2,1:T(2,128)(2,1)} %bitcast.852), channel_id=1, source_target_pairs={{0,2},{1,3},{2,4},{3,5},{4,6},{5,7},{8,10},{9,11},{10,12},{11,13},... | collective-permute-start | bytes 6291464 | tf_op jit(solution)/shard_map/ppermute | solution.py:15
  71.2 94.5 %collective-permute-start.1 = (bf16[2,2048,2,128]{3,0,2,1:T(2,128)(2,1)}, bf16[2,2048,2,128]{3,0,2,1:T(2,128)(2,1)}, u32[]{:S(2)}, u32[]{:S(2)}) collective-permute-start(bf16[2,2048,2,128]{3,0,2,1:T(2,128)(2,1)} %bitcast.853), channel_id=1, source_target_pairs={{0,1},{1,2},{2,3},{3,4},{4,5},{5,6},{6,7},{8,9},{9,10},{10,11},{11... | collective-permute-start | bytes 6291464 | tf_op jit(solution)/shard_map/ppermute | solution.py:15
  153.6 12.1 copy-start.2
  250.7 2.7 copy-start.9
  299.0 2.7 copy-start.9
  347.4 2.7 copy-start.9
  395.8 2.7 copy-start.9
  403.3 20.1 %copy-start.15 = (bf16[5,64,128]{2,1,0:T(8,128)(2,1)S(1)}, bf16[5,64,128]{2,1,0:T(8,128)(2,1)}, u32[]{:S(2)}) copy-start(bf16[5,64,128]{2,1,0:T(8,128)(2,1)} %get-tuple-element.3382) | copy-start | bytes 245764 | tf_op jit(solution)/shard_map/while
  444.0 2.7 copy-start.8
  450.5 20.1 %copy-start.15 = (bf16[5,64,128]{2,1,0:T(8,128)(2,1)S(1)}, bf16[5,64,128]{2,1,0:T(8,128)(2,1)}, u32[]{:S(2)}) copy-start(bf16[5,64,128]{2,1,0:T(8,128)(2,1)} %get-tuple-element.3382) | copy-start | bytes 245764 | tf_op jit(solution)/shard_map/while
  491.2 2.7 copy-start.8
  497.6 20.1 %copy-start.15 = (bf16[5,64,128]{2,1,0:T(8,128)(2,1)S(1)}, bf16[5,64,128]{2,1,0:T(8,128)(2,1)}, u32[]{:S(2)}) copy-start(bf16[5,64,128]{2,1,0:T(8,128)(2,1)} %get-tuple-element.3382) | copy-start | bytes 245764 | tf_op jit(solution)/shard_map/while
  538.3 2.7 copy-start.8
  544.7 20.1 %copy-start.15 = (bf16[5,64,128]{2,1,0:T(8,128)(2,1)S(1)}, bf16[5,64,128]{2,1,0:T(8,128)(2,1)}, u32[]{:S(2)}) copy-start(bf16[5,64,128]{2,1,0:T(8,128)(2,1)} %get-tuple-element.3382) | copy-start | bytes 245764 | tf_op jit(solution)/shard_map/while
  585.4 2.7 copy-start.8
  594.8 20.8 %copy-start.14 = (bf16[5,64,128]{2,1,0:T(8,128)(2,1)S(1)}, bf16[5,64,128]{2,1,0:T(8,128)(2,1)}, u32[]{:S(2)}) copy-start(bf16[5,64,128]{2,1,0:T(8,128)(2,1)} %get-tuple-element.3526) | copy-start | bytes 245764 | tf_op jit(solution)/shard_map/while
  637.1 2.7 copy-start.7
  643.6 20.8 %copy-start.14 = (bf16[5,64,128]{2,1,0:T(8,128)(2,1)S(1)}, bf16[5,64,128]{2,1,0:T(8,128)(2,1)}, u32[]{:S(2)}) copy-start(bf16[5,64,128]{2,1,0:T(8,128)(2,1)} %get-tuple-element.3526) | copy-start | bytes 245764 | tf_op jit(solution)/shard_map/while
  685.9 2.7 copy-start.7
  692.4 20.8 %copy-start.14 = (bf16[5,64,128]{2,1,0:T(8,128)(2,1)S(1)}, bf16[5,64,128]{2,1,0:T(8,128)(2,1)}, u32[]{:S(2)}) copy-start(bf16[5,64,128]{2,1,0:T(8,128)(2,1)} %get-tuple-element.3526) | copy-start | bytes 245764 | tf_op jit(solution)/shard_map/while
  734.7 2.7 copy-start.7
  741.3 20.8 %copy-start.14 = (bf16[5,64,128]{2,1,0:T(8,128)(2,1)S(1)}, bf16[5,64,128]{2,1,0:T(8,128)(2,1)}, u32[]{:S(2)}) copy-start(bf16[5,64,128]{2,1,0:T(8,128)(2,1)} %get-tuple-element.3526) | copy-start | bytes 245764 | tf_op jit(solution)/shard_map/while
  783.5 2.7 copy-start.7
  790.8 20.4 %copy-start.13 = (bf16[5,64,128]{2,1,0:T(8,128)(2,1)S(1)}, bf16[5,64,128]{2,1,0:T(8,128)(2,1)}, u32[]{:S(2)}) copy-start(bf16[5,64,128]{2,1,0:T(8,128)(2,1)} %get-tuple-element.3598) | copy-start | bytes 245764 | tf_op jit(solution)/shard_map/while
  838.4 20.4 %copy-start.13 = (bf16[5,64,128]{2,1,0:T(8,128)(2,1)S(1)}, bf16[5,64,128]{2,1,0:T(8,128)(2,1)}, u32[]{:S(2)}) copy-start(bf16[5,64,128]{2,1,0:T(8,128)(2,1)} %get-tuple-element.3598) | copy-start | bytes 245764 | tf_op jit(solution)/shard_map/while
  886.1 20.4 %copy-start.13 = (bf16[5,64,128]{2,1,0:T(8,128)(2,1)S(1)}, bf16[5,64,128]{2,1,0:T(8,128)(2,1)}, u32[]{:S(2)}) copy-start(bf16[5,64,128]{2,1,0:T(8,128)(2,1)} %get-tuple-element.3598) | copy-start | bytes 245764 | tf_op jit(solution)/shard_map/while
  933.8 20.4 %copy-start.13 = (bf16[5,64,128]{2,1,0:T(8,128)(2,1)S(1)}, bf16[5,64,128]{2,1,0:T(8,128)(2,1)}, u32[]{:S(2)}) copy-start(bf16[5,64,128]{2,1,0:T(8,128)(2,1)} %get-tuple-element.3598) | copy-start | bytes 245764 | tf_op jit(solution)/shard_map/while
  979.4 5.3 copy-start.19
  979.4 5.3 copy-start.23
  984.8 192.5 %copy-start.5 = (bf16[1,1,320,128]{3,2,1,0:T(8,128)(2,1)S(1)}, bf16[1,1,320,128]{3,2,1,0:T(8,128)(2,1)}, u32[]{:S(2)}) copy-start(bf16[1,1,320,128]{3,2,1,0:T(8,128)(2,1)} %get-tuple-element.1765) | copy-start | bytes 245764
  984.8 192.5 %copy-start.18 = (s32[1,5]{1,0:T(1,128)S(1)}, s32[1,5]{1,0:T(1,128)}, u32[]{:S(2)}) copy-start(s32[1,5]{1,0:T(1,128)} %get-tuple-element.3693) | copy-start | bytes 64
  984.8 192.5 %copy-start.22 = (s32[1,8]{1,0:T(1,128)S(1)}, s32[1,8]{1,0:T(1,128)}, u32[]{:S(2)}) copy-start(s32[1,8]{1,0:T(1,128)} %copy.432) | copy-start | bytes 100
  1028.7 2.7 copy-start.6
  1076.5 2.7 copy-start.6
  1124.4 2.7 copy-start.6
  1172.3 2.7 copy-start.6
  1177.3 196.9 %copy-start.17 = (s32[1,5]{1,0:T(1,128)S(1)}, s32[1,5]{1,0:T(1,128)}, u32[]{:S(2)}) copy-start(s32[1,5]{1,0:T(1,128)} %get-tuple-element.3765) | copy-start | bytes 64
  1177.3 196.9 %copy-start.21 = (s32[1,8]{1,0:T(1,128)S(1)}, s32[1,8]{1,0:T(1,128)}, u32[]{:S(2)}) copy-start(s32[1,8]{1,0:T(1,128)} %copy.433) | copy-start | bytes 100
  1179.7 21.0 %copy-start.12 = (bf16[5,64,128]{2,1,0:T(8,128)(2,1)S(1)}, bf16[5,64,128]{2,1,0:T(8,128)(2,1)}, u32[]{:S(2)}) copy-start(bf16[5,64,128]{2,1,0:T(8,128)(2,1)} %get-tuple-element.3742) | copy-start | bytes 245764 | tf_op jit(solution)/shard_map/while
  1228.7 21.0 %copy-start.12 = (bf16[5,64,128]{2,1,0:T(8,128)(2,1)S(1)}, bf16[5,64,128]{2,1,0:T(8,128)(2,1)}, u32[]{:S(2)}) copy-start(bf16[5,64,128]{2,1,0:T(8,128)(2,1)} %get-tuple-element.3742) | copy-start | bytes 245764 | tf_op jit(solution)/shard_map/while
  1277.6 21.0 %copy-start.12 = (bf16[5,64,128]{2,1,0:T(8,128)(2,1)S(1)}, bf16[5,64,128]{2,1,0:T(8,128)(2,1)}, u32[]{:S(2)}) copy-start(bf16[5,64,128]{2,1,0:T(8,128)(2,1)} %get-tuple-element.3742) | copy-start | bytes 245764 | tf_op jit(solution)/shard_map/while
  1326.6 21.0 %copy-start.12 = (bf16[5,64,128]{2,1,0:T(8,128)(2,1)S(1)}, bf16[5,64,128]{2,1,0:T(8,128)(2,1)}, u32[]{:S(2)}) copy-start(bf16[5,64,128]{2,1,0:T(8,128)(2,1)} %get-tuple-element.3742) | copy-start | bytes 245764 | tf_op jit(solution)/shard_map/while
  1374.1 197.3 %copy-start.3 = (bf16[1,1,320,128]{3,2,1,0:T(8,128)(2,1)S(1)}, bf16[1,1,320,128]{3,2,1,0:T(8,128)(2,1)}, u32[]{:S(2)}) copy-start(bf16[1,1,320,128]{3,2,1,0:T(8,128)(2,1)} %get-tuple-element.1761) | copy-start | bytes 245764
  1374.1 197.3 %copy-start.16 = (s32[1,5]{1,0:T(1,128)S(1)}, s32[1,5]{1,0:T(1,128)}, u32[]{:S(2)}) copy-start(s32[1,5]{1,0:T(1,128)} %get-tuple-element.3837) | copy-start | bytes 64
  1374.1 197.3 %copy-start.20 = (s32[1,8]{1,0:T(1,128)S(1)}, s32[1,8]{1,0:T(1,128)}, u32[]{:S(2)}) copy-start(s32[1,8]{1,0:T(1,128)} %copy.434) | copy-start | bytes 100
  1376.8 21.0 %copy-start.11 = (bf16[5,64,128]{2,1,0:T(8,128)(2,1)S(1)}, bf16[5,64,128]{2,1,0:T(8,128)(2,1)}, u32[]{:S(2)}) copy-start(bf16[5,64,128]{2,1,0:T(8,128)(2,1)} %get-tuple-element.3814) | copy-start | bytes 245764 | tf_op jit(solution)/shard_map/while
  1419.4 2.7 copy-start.4
  1425.8 21.0 %copy-start.11 = (bf16[5,64,128]{2,1,0:T(8,128)(2,1)S(1)}, bf16[5,64,128]{2,1,0:T(8,128)(2,1)}, u32[]{:S(2)}) copy-start(bf16[5,64,128]{2,1,0:T(8,128)(2,1)} %get-tuple-element.3814) | copy-start | bytes 245764 | tf_op jit(solution)/shard_map/while
  1468.4 2.7 copy-start.4
  1474.8 21.0 %copy-start.11 = (bf16[5,64,128]{2,1,0:T(8,128)(2,1)S(1)}, bf16[5,64,128]{2,1,0:T(8,128)(2,1)}, u32[]{:S(2)}) copy-start(bf16[5,64,128]{2,1,0:T(8,128)(2,1)} %get-tuple-element.3814) | copy-start | bytes 245764 | tf_op jit(solution)/shard_map/while
  1517.4 2.7 copy-start.4
  1523.9 21.0 %copy-start.11 = (bf16[5,64,128]{2,1,0:T(8,128)(2,1)S(1)}, bf16[5,64,128]{2,1,0:T(8,128)(2,1)}, u32[]{:S(2)}) copy-start(bf16[5,64,128]{2,1,0:T(8,128)(2,1)} %get-tuple-element.3814) | copy-start | bytes 245764 | tf_op jit(solution)/shard_map/while
  1566.4 2.7 copy-start.4
  1573.8 20.5 %copy-start.10 = (bf16[5,64,128]{2,1,0:T(8,128)(2,1)S(1)}, bf16[5,64,128]{2,1,0:T(8,128)(2,1)}, u32[]{:S(2)}) copy-start(bf16[5,64,128]{2,1,0:T(8,128)(2,1)} %get-tuple-element.3886) | copy-start | bytes 245764 | tf_op jit(solution)/shard_map/while
  1621.5 20.5 %copy-start.10 = (bf16[5,64,128]{2,1,0:T(8,128)(2,1)S(1)}, bf16[5,64,128]{2,1,0:T(8,128)(2,1)}, u32[]{:S(2)}) copy-start(bf16[5,64,128]{2,1,0:T(8,128)(2,1)} %get-tuple-element.3886) | copy-start | bytes 245764 | tf_op jit(solution)/shard_map/while
  1669.3 20.5 %copy-start.10 = (bf16[5,64,128]{2,1,0:T(8,128)(2,1)S(1)}, bf16[5,64,128]{2,1,0:T(8,128)(2,1)}, u32[]{:S(2)}) copy-start(bf16[5,64,128]{2,1,0:T(8,128)(2,1)} %get-tuple-element.3886) | copy-start | bytes 245764 | tf_op jit(solution)/shard_map/while
  1717.1 20.5 %copy-start.10 = (bf16[5,64,128]{2,1,0:T(8,128)(2,1)S(1)}, bf16[5,64,128]{2,1,0:T(8,128)(2,1)}, u32[]{:S(2)}) copy-start(bf16[5,64,128]{2,1,0:T(8,128)(2,1)} %get-tuple-element.3886) | copy-start | bytes 245764 | tf_op jit(solution)/shard_map/while
  1829.6 6.3 copy-start.1
Sparse Core Ops, SparseCore 0:
  66.5 67.5 all-reduce.9
where the time goes:
time: 1870 us; the launch traced here: 1840 us
  local copies, waits for them, and re-layouts  1330 us (71%)
  matrix products  210 us (11%)
  other arithmetic  125 us (7%)
  waiting for transfers between devices  84.3 us (5%)
  blocking collectives  41.5 us (2%)
  loops' own time  30.4 us (2%)
    gather x1536, local copies, waits for them, and re-layouts  1090 us
    dot_general x32, matrix products, attend_group(): jnp.einsum('mnop,ompj->mnj', slash_weights.astype(jnp.bfloat16), slash_va...  86.7 us
    reduce_sum x32, other arithmetic, attend_group(): jnp.sum(slash_weights, axis=(2, 3))  69.8 us
    psum x1, waiting for transfers between devices, per_device(): lax.psum(own_term, 'qblk').astype(jnp.float32).astype(jnp.bfloat16)  61 us
    dot_general x32, matrix products, attend_group(): jnp.einsum('pzf,opwf->pzow', query_block_list, slash_key_block, preferred...  56.8 us
    all_to_all x1, blocking collectives, per_device(): lax.all_to_all(stacked, 'head', split_axis=0, concat_axis=1, tiled=True)  41.5 us
    while x152, local copies, waits for them, and re-layouts  40.8 us
  transfers between devices with their start and end apart: 5, of which 3 were waited for; matrix products, arithmetic and copies ran while one was open for 3% of the time, Pallas kernels for 0%

commit v1 on v0

v1 whole, which is shorter than its diff:
```python
import functools
import math

import jax
import jax.numpy as jnp
from jax import lax
from jax.experimental import pallas as pl
from jax.experimental.pallas import tpu as pltpu
from jax.sharding import PartitionSpec as P

H = 32
KVH = 8
HD = 128
BLK = 64
MASKED = -1e30
VMEM_LIMIT = 48 * 1024 * 1024


def from_behind(value, axis, steps):
    count = lax.axis_size(axis)
    leading, last = (max(0, -steps), min(count, count - steps))
    return lax.ppermute(value, axis, [(source, source + steps) for source in range(leading, last)])


def pick_kernel(group, kv_heads, vert_count, offset_ref, kv_ref, out_ref):
    blocks = kv_ref.shape[0] // BLK
    q_heads = out_ref.shape[0] // (vert_count * BLK)
    for head in range(q_heads):
        k_col = (head // group) * HD
        v_col = (kv_heads + head // group) * HD
        for slot in range(vert_count):
            offset = offset_ref[head * vert_count + slot]
            inside = jnp.logical_and(offset >= 0, offset < blocks)
            start = pl.multiple_of(jnp.clip(offset, 0, blocks - 1) * BLK, BLK)
            row = (head * vert_count + slot) * BLK
            for place, col in ((0, k_col), (HD, v_col)):
                piece = kv_ref[pl.ds(start, BLK), col : col + HD]
                out_ref[row : row + BLK, place : place + HD] = jnp.where(
                    inside, piece, jnp.zeros_like(piece)
                )


def pick_vertical(kv_local, offsets, group, kv_heads):
    q_heads, vert_count = offsets.shape
    return pl.pallas_call(
        functools.partial(pick_kernel, group, kv_heads, vert_count),
        out_shape=jax.ShapeDtypeStruct((q_heads * vert_count * BLK, 2 * HD), kv_local.dtype),
        in_specs=[
            pl.BlockSpec(memory_space=pltpu.SMEM),
            pl.BlockSpec(memory_space=pltpu.VMEM),
        ],
        out_specs=pl.BlockSpec(memory_space=pltpu.VMEM),
        compiler_params=pltpu.CompilerParams(vmem_limit_bytes=VMEM_LIMIT),
        name="pick_vertical",
    )(offsets.reshape(-1), kv_local)


def attend_kernel(slash_ref, q_ref, k_ref, v_ref, vk_ref, vv_ref, bias_ref, out_ref):
    head = pl.program_id(0)
    slash_count = slash_ref.shape[1]
    blocks = q_ref.shape[0] // BLK
    front = k_ref.shape[0] // BLK - blocks
    scale = HD ** (-0.5) * math.log2(math.e)
    rows = lax.broadcasted_iota(jnp.int32, (BLK, 2 * BLK), 0)
    cols = lax.broadcasted_iota(jnp.int32, (BLK, 2 * BLK), 1)
    causal = jnp.where(jnp.logical_and(cols < BLK, cols > rows), MASKED, 0.0).astype(jnp.float32)
    offsets = [0] + [slash_ref[head, slot] for slot in range(slash_count)]
    vert_keys = vk_ref[...]
    vert_values = vv_ref[...]

    def one_block(block, carry):
        row = pl.multiple_of(block * BLK, BLK)
        starts = [pl.multiple_of((front + block - offset) * BLK, BLK) for offset in offsets]
        keys = jnp.concatenate([k_ref[pl.ds(start, BLK), :] for start in starts] + [vert_keys], 0)
        query = q_ref[pl.ds(row, BLK), :]
        scores = lax.dot_general(
            query, keys, (((1,), (1,)), ((), ())), preferred_element_type=jnp.float32
        )
        scores = scores * scale + bias_ref[0, pl.ds(block, 1), :]
        scores = jnp.concatenate([scores[:, : 2 * BLK] + causal, scores[:, 2 * BLK :]], 1)
        row_max = jnp.max(scores, axis=1, keepdims=True)
        weights = jnp.exp2(scores - row_max)
        row_total = jnp.sum(weights, axis=1, keepdims=True)
        values = jnp.concatenate(
            [v_ref[pl.ds(start, BLK), :] for start in starts] + [vert_values], 0
        )
        summed = jnp.dot(
            weights.astype(jnp.bfloat16), values, preferred_element_type=jnp.float32
        )
        out_ref[pl.ds(row, BLK), :] = (summed / row_total).astype(out_ref.dtype)
        return carry

    lax.fori_loop(0, blocks, one_block, 0, unroll=4)


def attend(queries, window, vertical, slash, bias, group, kv_heads):
    rows = queries.shape[0]
    q_heads, blocks, width = bias.shape
    front_rows = window.shape[0]
    vert_rows = vertical.shape[0] // q_heads
    products = 4 * q_heads * rows * width * HD
    return pl.pallas_call(
        attend_kernel,
        out_shape=jax.ShapeDtypeStruct((rows, q_heads * HD), queries.dtype),
        grid_spec=pltpu.PrefetchScalarGridSpec(
            num_scalar_prefetch=1,
            grid=(q_heads,),
            in_specs=[
                pl.BlockSpec((rows, HD), lambda h, s: (0, h)),
                pl.BlockSpec((front_rows, HD), lambda h, s: (0, h // group)),
                pl.BlockSpec((front_rows, HD), lambda h, s: (0, kv_heads + h // group)),
                pl.BlockSpec((vert_rows, HD), lambda h, s: (h, 0)),
                pl.BlockSpec((vert_rows, HD), lambda h, s: (h, 1)),
                pl.BlockSpec((1, blocks, width), lambda h, s: (h, 0, 0)),
            ],
            out_specs=pl.BlockSpec((rows, HD), lambda h, s: (0, h)),
        ),
        compiler_params=pltpu.CompilerParams(
            dimension_semantics=("arbitrary",), vmem_limit_bytes=VMEM_LIMIT
        ),
        cost_estimate=pl.CostEstimate(
            flops=products,
            bytes_accessed=4 * rows * q_heads * HD + 2 * window.size,
            transcendentals=q_heads * rows * width,
        ),
        name="attend",
    )(slash, queries, window, window, vertical, vertical, bias)


def per_device(queries, key_states, value_states, vertical_blocks, slash_offsets):
    head_count = lax.axis_size("head")
    head_index = lax.axis_index("head")
    block_index = lax.axis_index("qblk")
    rows_in = queries.shape[0]
    q_heads = H // head_count
    copies = max(1, head_count // KVH)
    kv_heads = KVH * copies // head_count
    group = q_heads // kv_heads

    def by_head(states):
        split = states.reshape(rows_in, KVH, HD)
        if copies > 1:
            split = jnp.repeat(split, copies, axis=1)
        return split.reshape(rows_in, head_count, kv_heads * HD)

    kv_pair = jnp.concatenate([by_head(key_states), by_head(value_states)], axis=2)
    kv_pair = kv_pair.reshape(rows_in, head_count * 2 * kv_heads * HD)
    kv_local = lax.all_to_all(kv_pair, "head", split_axis=1, concat_axis=0, tiled=True)
    row_count = kv_local.shape[0]
    blocks = row_count // BLK

    vert_mine = lax.dynamic_slice_in_dim(vertical_blocks, head_index * q_heads, q_heads, 0)
    slash_mine = lax.dynamic_slice_in_dim(slash_offsets, head_index * q_heads, q_heads, 0)
    first_block = block_index * blocks
    own_vertical = pick_vertical(kv_local, vert_mine - first_block, group, kv_heads)
    vertical = lax.psum(own_vertical, "qblk")
    two_back = from_behind(kv_local, "qblk", 2)
    one_back = from_behind(kv_local, "qblk", 1)

    block_ids = first_block + jnp.arange(blocks, dtype=jnp.int32)
    slash_ok = block_ids[None, :, None] - slash_mine[:, None, :] >= 0
    block_gap = block_ids[None, :, None] - vert_mine[:, None, :]
    slash_hit = jnp.any(block_gap[:, :, :, None] == slash_mine[:, None, None, :], axis=3)
    vert_ok = (block_gap > 0) & jnp.logical_not(slash_hit)
    allowed = jnp.concatenate([jnp.ones((q_heads, blocks, 1), bool), slash_ok, vert_ok], axis=2)
    bias = jnp.where(allowed, 0.0, MASKED).astype(jnp.float32)
    bias = jnp.broadcast_to(bias[:, :, :, None], bias.shape + (BLK,))
    bias = bias.reshape(q_heads, blocks, -1)

    q_local = lax.all_to_all(queries, "head", split_axis=1, concat_axis=0, tiled=True)
    window = jnp.concatenate([two_back, one_back, kv_local], axis=0)
    attended = attend(q_local, window, vertical, slash_mine, bias, group, kv_heads)
    return lax.all_to_all(attended, "head", split_axis=0, concat_axis=1, tiled=True)


def solution(mesh):
    return jax.shard_map(
        per_device,
        mesh=mesh,
        in_specs=(
            P(("qblk", "head"), None),
            P(("qblk", "head"), None),
            P(("qblk", "head"), None),
            P(),
            P(),
        ),
        out_specs=P(("qblk", "head"), None),
        check_vma=False,
    )
```

time: 1870 us -> 286 us (0.15)
  the two profiles are of different devices: /device:TPU:24 before, /device:TPU:1 now
where the time goes in v1:
time: 286 us; the launch traced here: 285 us
  waiting for transfers between devices  100 us (35%)
  Pallas kernels  99 us (35%)
  blocking collectives  31.7 us (11%)
  starting transfers between devices  18.6 us (7%)
  local copies, waits for them, and re-layouts  14.7 us (5%)
  between operations  13.5 us (5%)
  other arithmetic  7.53 us (3%)
    pallas_call x1, Pallas kernels, attend(): pl.pallas_call(attend_kernel, out_shape=jax.ShapeDtypeStruct((rows, q_hea...  97 us
    ppermute x2, waiting for transfers between devices, from_behind(): lax.ppermute(value, axis, [(source, source + steps) for source in range(l...  80.8 us
    all_to_all x1, blocking collectives, per_device(): lax.all_to_all(attended, 'head', split_axis=0, concat_axis=1, tiled=True)  31.7 us
    all_to_all x1, waiting for transfers between devices, per_device(): lax.all_to_all(kv_pair, 'head', split_axis=1, concat_axis=0, tiled=True)  19.5 us
    ppermute x2, starting transfers between devices, from_behind(): lax.ppermute(value, axis, [(source, source + steps) for source in range(l...  9.26 us
  transfers between devices with their start and end apart: 5, of which 3 were waited for; matrix products, arithmetic and copies ran while one was open for 5% of the time, Pallas kernels for 1%

profile of v1, /device:TPU:1, one launch (start us, length us, event | category | flops | bytes accessed | tf_op | source)
XLA Modules:
  0.0 285.4 jit_solution(5802105200312094710)
XLA Ops:
  6.5 0.0 copy-start
  6.5 1.7 copy_bitcast_fusion.1
  8.2 1.5 pad_maximum_fusion.1
  9.8 4.3 %all-to-all-start.1 = ((bf16[512,4,512]{2,0,1:T(8,128)(2,1)}), bf16[512,4,512]{2,0,1:T(8,128)(2,1)S(1)}, u32[]{:S(2)}, u32[]{:S(2)}) async-start(bf16[512,4,512]{2,0,1:T(8,128)(2,1)} %pad_maximum_fusion.1), calls=%async_computation.1 | async-start | bytes 4194304 | tf_op jit(solution)/shard_map/all_to_all | solution.py:148
  14.0 4.8 %copy.47 = bf16[64,4,8,1024]{3,2,0,1:T(8,128)(2,1)} copy(bf16[64,4,8,1024]{3,2,1,0:T(8,128)(2,1)} %bitcast.27) | data formatting | bytes 8388608 | tf_op jit(solution)/shard_map/all_to_all | solution.py:170
  18.8 19.5 %all-to-all-done.1 = bf16[512,4,512]{2,0,1:T(8,128)(2,1)S(1)} async-done(((bf16[512,4,512]{2,0,1:T(8,128)(2,1)}), bf16[512,4,512]{2,0,1:T(8,128)(2,1)S(1)}, u32[]{:S(2)}, u32[]{:S(2)}) %all-to-all-start.1) | async-done | bytes 2097184 | tf_op jit(solution)/shard_map/all_to_all | solution.py:148
  38.4 0.0 copy-start.2
  38.4 5.0 %all-to-all-start = ((bf16[512,4,1024]{2,0,1:T(8,128)(2,1)}), bf16[512,4,1024]{2,0,1:T(8,128)(2,1)}, u32[]{:S(2)}, u32[]{:S(2)}) async-start(bf16[512,4,1024]{2,0,1:T(8,128)(2,1)} %bitcast.25), calls=%async_computation | async-start | bytes 8388608 | tf_op jit(solution)/shard_map/all_to_all | solution.py:170
  43.4 0.0 all-reduce.2.cloned.1.call-start
  43.4 4.7 %collective-permute-start.1 = (bf16[2048,512]{1,0:T(8,128)(2,1)S(1)}, bf16[2048,512]{1,0:T(8,128)(2,1)}, u32[]{:S(2)}, u32[]{:S(2)}) collective-permute-start(bf16[2048,512]{1,0:T(8,128)(2,1)S(1)} %bitcast.21), channel_id=1, source_target_pairs={{0,1},{1,2},{2,3},{3,4},{4,5},{5,6},{6,7},{8,9},{9,10},{10,11},{11... | collective-permute-start | bytes 6291464 | tf_op jit(solution)/shard_map/ppermute | solution.py:22
  48.1 4.5 %collective-permute-start = (bf16[2048,512]{1,0:T(8,128)(2,1)S(1)}, bf16[2048,512]{1,0:T(8,128)(2,1)}, u32[]{:S(2)}, u32[]{:S(2)}) collective-permute-start(bf16[2048,512]{1,0:T(8,128)(2,1)S(1)} %bitcast.22), channel_id=1, source_target_pairs={{0,2},{1,3},{2,4},{3,5},{4,6},{5,7},{8,10},{9,11},{10,12},{11,13},... | collective-permute-start | bytes 6291464 | tf_op jit(solution)/shard_map/ppermute | solution.py:22
  52.7 0.0 copy-done
  52.7 0.1 constant_dynamic-slice_fusion.1
  52.8 0.1 copy.39.slash_ref
  52.8 0.0 copy-done.2
  52.8 0.1 broadcast_subtract_fusion.1
  52.9 0.1 copy.33
  53.0 0.1 reshape.41.offset_ref
  53.1 0.1 copy.35
  53.2 0.1 broadcast_subtract_fusion
  53.2 0.1 compare_reduce_fusion
  53.4 0.1 not_and_fusion
  53.5 0.1 subtract_compare_fusion
  53.6 0.1 add_select_fusion
  53.7 0.1 copy.37
  53.8 2.0 broadcast_in_dim.26
  55.7 2.0 reshape.42.bias_ref
  57.8 2.0 pick_vertical.1
  59.8 0.0 all-reduce.2.cloned.1.call-update
  59.8 48.6 %collective-permute-done.1 = bf16[2048,512]{1,0:T(8,128)(2,1)} collective-permute-done((bf16[2048,512]{1,0:T(8,128)(2,1)S(1)}, bf16[2048,512]{1,0:T(8,128)(2,1)}, u32[]{:S(2)}, u32[]{:S(2)}) %collective-permute-start.1) | collective-permute-done | bytes 2097184 | tf_op jit(solution)/shard_map/ppermute | solution.py:22
  108.3 32.3 %collective-permute-done = bf16[2048,512]{1,0:T(8,128)(2,1)} collective-permute-done((bf16[2048,512]{1,0:T(8,128)(2,1)S(1)}, bf16[2048,512]{1,0:T(8,128)(2,1)}, u32[]{:S(2)}, u32[]{:S(2)}) %collective-permute-start) | collective-permute-done | bytes 2097184 | tf_op jit(solution)/shard_map/ppermute | solution.py:22
  140.6 5.5 %pad_maximum_fusion.k_ref.v_ref = bf16[6144,512]{1,0:T(8,128)(2,1)} fusion(bf16[2048,512]{1,0:T(8,128)(2,1)S(1)} %bitcast.24, bf16[2048,512]{1,0:T(8,128)(2,1)} %collective-permute-done.1, bf16[2048,512]{1,0:T(8,128)(2,1)} %collective-permute-done), kind=kLoop, calls=%fused_computation | loop fusion | flops 18874368 | bytes 12582912 | tf_op jit(solution)/shard_map/concatenate | solution.py:171
  146.1 0.0 all-reduce.2.cloned.1.call-done.vk_ref.vv_ref
  146.1 0.0 all-to-all-done
  146.1 0.0 copy-start.1
  146.1 1.3 copy-done.1
  147.4 97.0 %attend.1 = bf16[2048,1024]{1,0:T(8,128)(2,1)} custom-call(s32[8,8]{1,0:T(8,128)S(1)} %copy.39.slash_ref, bf16[2048,1024]{1,0:T(8,128)(2,1)} %bitcast.1.q_ref, bf16[6144,512]{1,0:T(8,128)(2,1)} %pad_maximum_fusion.k_ref.v_ref, bf16[6144,512]{1,0:T(8,128)(2,1)} %pad_maximum_fusion.k_ref.v_ref, bf16[2560,256]{1,0:T(8,128)(2,1)S(1)} %copy-done.1, ...), custom_call_target="tpu_custom_call" | custom-call | flops 7516192768 | bytes 14680064 | tf_op jit(solution)/shard_map/attend/pallas_call | solution.py:102
  244.4 31.7 %all_to_all.54 = bf16[4,512,1024]{2,1,0:T(8,128)(2,1)S(1)} all-to-all(bf16[4,512,1024]{2,1,0:T(8,128)(2,1)} %bitcast.28), channel_id=1, replica_groups=mesh['head'=4,'qblk'=8] {'head'}, dimensions={0} | all-to-all | bytes 8388608 | tf_op jit(solution)/shard_map/all_to_all | solution.py:173
  276.1 2.5 copy.43
  (3 shorter events, 0.0 us)
Async XLA Ops:
  6.5 46.1 %copy-start = (s32[32,8]{0,1:T(8,128)S(1)}, s32[32,8]{0,1:T(8,128)}, u32[]{:S(2)}) copy-start(s32[32,8]{0,1:T(8,128)} %param.9) | copy-start | bytes 3076
  9.8 28.6 %all-to-all-start.1 = ((bf16[512,4,512]{2,0,1:T(8,128)(2,1)}), bf16[512,4,512]{2,0,1:T(8,128)(2,1)S(1)}, u32[]{:S(2)}, u32[]{:S(2)}) async-start(bf16[512,4,512]{2,0,1:T(8,128)(2,1)} %pad_maximum_fusion.1), calls=%async_computation.1 | async-start | bytes 4194304 | tf_op jit(solution)/shard_map/all_to_all | solution.py:148
  38.4 14.5 %copy-start.2 = (s32[32,5]{0,1:T(8,128)S(1)}, s32[32,5]{0,1:T(8,128)}, u32[]{:S(2)}) copy-start(s32[32,5]{0,1:T(8,128)} %param.8) | copy-start | bytes 1924
  38.4 107.7 %all-to-all-start = ((bf16[512,4,1024]{2,0,1:T(8,128)(2,1)}), bf16[512,4,1024]{2,0,1:T(8,128)(2,1)}, u32[]{:S(2)}, u32[]{:S(2)}) async-start(bf16[512,4,1024]{2,0,1:T(8,128)(2,1)} %bitcast.25), calls=%async_computation | async-start | bytes 8388608 | tf_op jit(solution)/shard_map/all_to_all | solution.py:170
  43.4 102.7 %all-reduce.2.cloned.1.call-start = ((), (), s32[]{:S(2)}) async-start(), calls=%async_computation.3 | async-start | bytes 2621440 | tf_op jit(solution)/shard_map/psum | solution.py:156
  43.4 64.9 %collective-permute-start.1 = (bf16[2048,512]{1,0:T(8,128)(2,1)S(1)}, bf16[2048,512]{1,0:T(8,128)(2,1)}, u32[]{:S(2)}, u32[]{:S(2)}) collective-permute-start(bf16[2048,512]{1,0:T(8,128)(2,1)S(1)} %bitcast.21), channel_id=1, source_target_pairs={{0,1},{1,2},{2,3},{3,4},{4,5},{5,6},{6,7},{8,9},{9,10},{10,11},{11... | collective-permute-start | bytes 6291464 | tf_op jit(solution)/shard_map/ppermute | solution.py:22
  48.1 92.5 %collective-permute-start = (bf16[2048,512]{1,0:T(8,128)(2,1)S(1)}, bf16[2048,512]{1,0:T(8,128)(2,1)}, u32[]{:S(2)}, u32[]{:S(2)}) collective-permute-start(bf16[2048,512]{1,0:T(8,128)(2,1)S(1)} %bitcast.22), channel_id=1, source_target_pairs={{0,2},{1,3},{2,4},{3,5},{4,6},{5,7},{8,10},{9,11},{10,12},{11,13},... | collective-permute-start | bytes 6291464 | tf_op jit(solution)/shard_map/ppermute | solution.py:22
  146.1 1.3 copy-start.1
Sparse Core Ops, SparseCore 0:
  59.9 62.9 all-reduce.1

commit v2 on v1

v2 whole, which is shorter than its diff:
```python
import functools
import math

import jax
import jax.numpy as jnp
from jax import lax
from jax.experimental import pallas as pl
from jax.experimental.pallas import tpu as pltpu
from jax.sharding import PartitionSpec as P

H = 32
KVH = 8
HD = 128
BLK = 64
MASKED = -1e30
VMEM_LIMIT = 48 * 1024 * 1024


def from_behind(value, axis, steps):
    count = lax.axis_size(axis)
    leading, last = (max(0, -steps), min(count, count - steps))
    return lax.ppermute(value, axis, [(source, source + steps) for source in range(leading, last)])


def pick_kernel(vert_count, offset_ref, kv_ref, out_ref):
    blocks = kv_ref.shape[0] // BLK
    for slot in range(out_ref.shape[0] // BLK):
        offset = offset_ref[slot]
        inside = jnp.logical_and(offset >= 0, offset < blocks)
        start = pl.multiple_of(jnp.clip(offset, 0, blocks - 1) * BLK, BLK)
        piece = kv_ref[pl.ds(start, BLK), :]
        out_ref[slot * BLK : (slot + 1) * BLK, :] = jnp.where(
            inside, piece, jnp.zeros_like(piece)
        )


def pick_vertical(kv_local, offsets):
    q_heads, vert_count = offsets.shape
    return pl.pallas_call(
        functools.partial(pick_kernel, vert_count),
        out_shape=jax.ShapeDtypeStruct((q_heads * vert_count * BLK, 2 * HD), kv_local.dtype),
        in_specs=[
            pl.BlockSpec(memory_space=pltpu.SMEM),
            pl.BlockSpec(memory_space=pltpu.VMEM),
        ],
        out_specs=pl.BlockSpec(memory_space=pltpu.VMEM),
        compiler_params=pltpu.CompilerParams(vmem_limit_bytes=VMEM_LIMIT),
        name="pick_vertical",
    )(offsets.reshape(-1), kv_local)


def attend_kernel(
    slash_ref,
    odd_ref,
    q_ref,
    two_ref,
    low_ref,
    high_ref,
    own_ref,
    vert_ref,
    bias_ref,
    out_ref,
    window_ref,
):
    head = pl.program_id(0)
    slash_count = slash_ref.shape[1]
    rows = q_ref.shape[0]
    blocks = rows // BLK
    front = 2 * blocks

    @pl.when(head == 0)
    def _():
        window_ref[:rows, :] = two_ref[...]
        window_ref[2 * rows :, :] = own_ref[...]

        @pl.when(odd_ref[0] == 1)
        def _():
            window_ref[rows : 2 * rows, :] = low_ref[...]

        @pl.when(odd_ref[0] == 0)
        def _():
            window_ref[rows : 2 * rows, :] = high_ref[...]

    scale = HD ** (-0.5) * math.log2(math.e)
    row_ids = lax.broadcasted_iota(jnp.int32, (BLK, 2 * BLK), 0)
    col_ids = lax.broadcasted_iota(jnp.int32, (BLK, 2 * BLK), 1)
    hidden = jnp.logical_and(col_ids < BLK, col_ids > row_ids)
    causal = jnp.where(hidden, MASKED, 0.0).astype(jnp.float32)
    offsets = [0] + [slash_ref[head, slot] for slot in range(slash_count)]
    lead = (1 + slash_count) % 2 * BLK
    split = (1 + slash_count) * BLK + lead
    together = 4 if blocks % 4 == 0 else 1

    def one_group(step, carry):
        base = pl.multiple_of(step * together * BLK, BLK)
        shared = lax.dot_general(
            q_ref[pl.ds(base, together * BLK), :],
            vert_ref[lead:, :HD],
            (((1,), (1,)), ((), ())),
            preferred_element_type=jnp.float32,
        )
        sums, totals, shared_weights = [], [], []
        for part in range(together):
            block = step * together + part
            row = pl.multiple_of(block * BLK, BLK)
            starts = [pl.multiple_of((front + block - offset) * BLK, BLK) for offset in offsets]

            def gathered(first):
                pieces = [window_ref[pl.ds(start, BLK), first : first + HD] for start in starts]
                if lead:
                    pieces.append(vert_ref[:lead, first : first + HD])
                return jnp.concatenate(pieces, 0)

            scores = lax.dot_general(
                q_ref[pl.ds(row, BLK), :],
                gathered(0),
                (((1,), (1,)), ((), ())),
                preferred_element_type=jnp.float32,
            )
            scores = scores * scale + bias_ref[0, pl.ds(block, 1), :split]
            scores = jnp.concatenate([scores[:, : 2 * BLK] + causal, scores[:, 2 * BLK :]], 1)
            vert_scores = shared[part * BLK : (part + 1) * BLK] * scale
            vert_scores = vert_scores + bias_ref[0, pl.ds(block, 1), split:]
            row_max = jnp.maximum(
                jnp.max(scores, axis=1, keepdims=True),
                jnp.max(vert_scores, axis=1, keepdims=True),
            )
            weights = jnp.exp2(scores - row_max)
            vert_weights = jnp.exp2(vert_scores - row_max)
            totals.append(
                jnp.sum(weights, axis=1, keepdims=True)
                + jnp.sum(vert_weights, axis=1, keepdims=True)
            )
            shared_weights.append(vert_weights.astype(jnp.bfloat16))
            sums.append(
                jnp.dot(
                    weights.astype(jnp.bfloat16), gathered(HD), preferred_element_type=jnp.float32
                )
            )
        summed = jnp.dot(
            jnp.concatenate(shared_weights, 0),
            vert_ref[lead:, HD:],
            preferred_element_type=jnp.float32,
        )
        summed = summed + jnp.concatenate(sums, 0)
        out_ref[pl.ds(base, together * BLK), :] = (
            summed / jnp.concatenate(totals, 0)
        ).astype(out_ref.dtype)
        return carry

    lax.fori_loop(0, blocks // together, one_group, 0, unroll=2)


def attend(queries, two_back, low, high, own, odd, vertical, slash, bias):
    rows = queries.shape[0]
    q_heads, blocks, width = bias.shape
    vert_rows = vertical.shape[0] // q_heads
    whole = pl.BlockSpec((rows, 2 * HD), lambda h, s, o: (0, 0))
    return pl.pallas_call(
        attend_kernel,
        out_shape=jax.ShapeDtypeStruct((rows, q_heads * HD), queries.dtype),
        grid_spec=pltpu.PrefetchScalarGridSpec(
            num_scalar_prefetch=2,
            grid=(q_heads,),
            in_specs=[
                pl.BlockSpec((rows, HD), lambda h, s, o: (0, h)),
                whole,
                whole,
                whole,
                whole,
                pl.BlockSpec((vert_rows, 2 * HD), lambda h, s, o: (h, 0)),
                pl.BlockSpec((1, blocks, width), lambda h, s, o: (h, 0, 0)),
            ],
            out_specs=pl.BlockSpec((rows, HD), lambda h, s, o: (0, h)),
            scratch_shapes=[pltpu.VMEM((3 * rows, 2 * HD), queries.dtype)],
        ),
        compiler_params=pltpu.CompilerParams(
            dimension_semantics=("arbitrary",), vmem_limit_bytes=VMEM_LIMIT
        ),
        cost_estimate=pl.CostEstimate(
            flops=4 * q_heads * rows * width * HD,
            bytes_accessed=4 * q_heads * blocks * width * HD,
            transcendentals=q_heads * rows * width,
        ),
        name="attend",
    )(slash, odd, queries, two_back, low, high, own, vertical, bias)


def per_device(queries, key_states, value_states, vertical_blocks, slash_offsets):
    head_count = lax.axis_size("head")
    head_index = lax.axis_index("head")
    run_count = lax.axis_size("qblk")
    block_index = lax.axis_index("qblk")
    rows_in = queries.shape[0]
    q_heads = H // head_count
    copies = max(1, head_count // KVH)
    kv_heads = KVH * copies // head_count
    group = q_heads // kv_heads

    wide = group * HD

    def columns(array, first, width):
        return lax.slice_in_dim(array, first, first + width, axis=1)

    def to_heads(pieces):
        flat = jnp.concatenate(pieces, axis=1)
        return lax.all_to_all(flat, "head", split_axis=1, concat_axis=0, tiled=True)

    own = [
        to_heads(
            [
                columns(states, (peer * kv_heads + kv) // copies * HD, HD)
                for peer in range(head_count)
                for states in (key_states, value_states)
            ]
        )
        for kv in range(kv_heads)
    ]
    row_count = own[0].shape[0]
    blocks = row_count // BLK
    vert_mine = lax.dynamic_slice_in_dim(vertical_blocks, head_index * q_heads, q_heads, 0)
    slash_mine = lax.dynamic_slice_in_dim(slash_offsets, head_index * q_heads, q_heads, 0)
    first_block = block_index * blocks
    odd = lax.rem(block_index, 2).astype(jnp.int32).reshape(1)

    block_ids = first_block + jnp.arange(blocks, dtype=jnp.int32)
    slash_ok = block_ids[None, :, None] - slash_mine[:, None, :] >= 0
    block_gap = block_ids[None, :, None] - vert_mine[:, None, :]
    slash_hit = jnp.any(block_gap[:, :, :, None] == slash_mine[:, None, None, :], axis=3)
    vert_ok = (block_gap > 0) & jnp.logical_not(slash_hit)
    allowed = jnp.concatenate([jnp.ones((q_heads, blocks, 1), bool), slash_ok, vert_ok], axis=2)
    bias = jnp.where(allowed, 0.0, MASKED).astype(jnp.float32)
    bias = jnp.broadcast_to(bias[:, :, :, None], bias.shape + (BLK,))
    bias = bias.reshape(q_heads, blocks, -1)

    upward = [(run, run + 1) for run in range(0, run_count - 1, 2)]
    downward = [(run + 1, run) for run in range(0, run_count - 1, 2)]
    returned = []
    for kv in range(kv_heads):
        heads = slice(kv * group, (kv + 1) * group)
        two_back = from_behind(own[kv], "qblk", 2)
        vertical = lax.psum(pick_vertical(own[kv], vert_mine[heads] - first_block), "qblk")
        low = lax.ppermute(own[kv], "qblk", upward)
        q_local = to_heads(
            [columns(queries, (peer * kv_heads + kv) * wide, wide) for peer in range(head_count)]
        )
        high = lax.ppermute(two_back, "qblk", downward)
        attended = attend(
            q_local, two_back, low, high, own[kv], odd, vertical, slash_mine[heads], bias[heads]
        )
        returned.append(
            lax.all_to_all(attended, "head", split_axis=0, concat_axis=1, tiled=True)
        )
    return jnp.concatenate(
        [columns(part, peer * wide, wide) for peer in range(head_count) for part in returned], 1
    )


def solution(mesh):
    return jax.shard_map(
        per_device,
        mesh=mesh,
        in_specs=(
            P(("qblk", "head"), None),
            P(("qblk", "head"), None),
            P(("qblk", "head"), None),
            P(),
            P(),
        ),
        out_specs=P(("qblk", "head"), None),
        check_vma=False,
    )
```

time: 286 us -> 315 us (1.10)
  the two profiles are of different devices: /device:TPU:1 before, /device:TPU:24 now
where the time goes in v2:
time: 315 us; the launch traced here: 310 us
  waiting for transfers between devices  127 us (40%)
  Pallas kernels  100 us (32%)
  starting transfers between devices  34 us (11%)
  local copies, waits for them, and re-layouts  32.4 us (10%)
  between operations  13.7 us (4%)
    pallas_call x2, Pallas kernels, attend(): pl.pallas_call(attend_kernel, out_shape=jax.ShapeDtypeStruct((rows, q_hea...  97.2 us
    psum x1, waiting for transfers between devices, per_device(): lax.psum(pick_vertical(own[kv], vert_mine[heads] - first_block), 'qblk')  63.8 us
    all_to_all x4, waiting for transfers between devices, to_heads(): return lax.all_to_all(flat, 'head', split_axis=1, concat_axis=0, tiled=True)  39 us
    all_to_all x2, waiting for transfers between devices, per_device(): lax.all_to_all(attended, 'head', split_axis=0, concat_axis=1, tiled=True)  23.7 us
    all_to_all x4, starting transfers between devices, to_heads(): return lax.all_to_all(flat, 'head', split_axis=1, concat_axis=0, tiled=True)  16.1 us
    unnamed x25, local copies, waits for them, and re-layouts  10.9 us
    all_to_all x2, starting transfers between devices, per_device(): lax.all_to_all(attended, 'head', split_axis=0, concat_axis=1, tiled=True)  9.04 us
    all_to_all x4, local copies, waits for them, and re-layouts, to_heads(): return lax.all_to_all(flat, 'head', split_axis=1, concat_axis=0, tiled=True)  6.76 us
  transfers between devices with their start and end apart: 13, of which 6 were waited for; matrix products, arithmetic and copies ran while one was open for 6% of the time, Pallas kernels for 32%

profile of v2, /device:TPU:24, one launch (start us, length us, event | category | flops | bytes accessed | tf_op | source)
XLA Modules:
  0.0 309.6 jit_solution(2705458021903995344)
XLA Ops:
  6.5 1.0 slice_dynamic-update-slice_fusion.15
  7.6 1.1 slice_dynamic-update-slice_fusion.14
  8.7 1.1 slice_dynamic-update-slice_fusion.13
  9.7 1.1 slice_dynamic-update-slice_fusion.12
  10.8 1.1 slice_dynamic-update-slice_fusion.11
  11.9 1.1 slice_dynamic-update-slice_fusion.10
  12.9 1.1 slice_dynamic-update-slice_fusion.9
  14.0 1.1 slice_dynamic-update-slice_fusion.8
  15.1 1.0 copy.67
  16.1 3.7 %all-to-all-start.1 = ((bf16[512,4,256]{2,0,1:T(8,128)(2,1)}), bf16[512,4,256]{2,0,1:T(8,128)(2,1)S(1)}, u32[]{:S(2)}, u32[]{:S(2)}) async-start(bf16[512,4,256]{2,0,1:T(8,128)(2,1)} %bitcast.45), calls=%async_computation.1 | async-start | bytes 2097152 | tf_op jit(solution)/shard_map/all_to_all | solution.py:207
  19.8 1.1 copy.66
  20.9 12.6 %all-to-all-done.1 = bf16[512,4,256]{2,0,1:T(8,128)(2,1)S(1)} async-done(((bf16[512,4,256]{2,0,1:T(8,128)(2,1)}), bf16[512,4,256]{2,0,1:T(8,128)(2,1)S(1)}, u32[]{:S(2)}, u32[]{:S(2)}) %all-to-all-start.1) | async-done | bytes 1048608 | tf_op jit(solution)/shard_map/all_to_all | solution.py:207
  33.5 3.5 %all-to-all-start.4 = ((bf16[512,4,256]{2,0,1:T(8,128)(2,1)}), bf16[512,4,256]{2,0,1:T(8,128)(2,1)S(1)}, u32[]{:S(2)}, u32[]{:S(2)}) async-start(bf16[512,4,256]{2,0,1:T(8,128)(2,1)} %bitcast.44), calls=%async_computation.4 | async-start | bytes 2097152 | tf_op jit(solution)/shard_map/all_to_all | solution.py:207
  37.0 2.6 fusion.1
  39.7 1.6 pad_maximum_fusion
  41.3 1.5 copy.64
  42.9 7.2 %all-to-all-done.4 = bf16[512,4,256]{2,0,1:T(8,128)(2,1)S(1)} async-done(((bf16[512,4,256]{2,0,1:T(8,128)(2,1)}), bf16[512,4,256]{2,0,1:T(8,128)(2,1)S(1)}, u32[]{:S(2)}, u32[]{:S(2)}) %all-to-all-start.4) | async-done | bytes 1048608 | tf_op jit(solution)/shard_map/all_to_all | solution.py:207
  50.1 4.5 %all-to-all-start.3 = ((bf16[512,4,512]{2,0,1:T(8,128)(2,1)}), bf16[512,4,512]{2,0,1:T(8,128)(2,1)}, u32[]{:S(2)}, u32[]{:S(2)}) async-start(bf16[512,4,512]{2,0,1:T(8,128)(2,1)} %bitcast.63), calls=%async_computation.3 | async-start | bytes 4194304 | tf_op jit(solution)/shard_map/all_to_all | solution.py:207
  54.6 1.3 collective-permute-start.3
  55.9 0.1 constant_dynamic-slice_fusion
  56.0 0.1 copy.44
  56.0 0.1 slice_subtract_fusion
  56.1 0.1 copy.42
  56.2 0.1 reshape.68.offset_ref
  56.3 0.1 copy.50
  56.4 0.1 reshape.69.offset_ref
  56.5 0.1 constant_dynamic-slice_fusion.1
  56.6 0.1 copy.53
  56.6 3.1 %copy.65 = bf16[64,4,8,512]{3,2,0,1:T(8,128)(2,1)} copy(bf16[64,4,8,512]{3,2,1,0:T(8,128)(2,1)} %bitcast.64) | data formatting | bytes 4194304 | tf_op jit(solution)/shard_map/all_to_all | solution.py:207
  59.8 0.1 broadcast_subtract_fusion
  59.8 19.1 %all-to-all-done.3 = bf16[512,4,512]{2,0,1:T(8,128)(2,1)} async-done(((bf16[512,4,512]{2,0,1:T(8,128)(2,1)}), bf16[512,4,512]{2,0,1:T(8,128)(2,1)}, u32[]{:S(2)}, u32[]{:S(2)}) %all-to-all-start.3) | async-done | bytes 2097184 | tf_op jit(solution)/shard_map/all_to_all | solution.py:207
  78.9 4.4 %all-to-all-start = ((bf16[512,4,512]{2,0,1:T(8,128)(2,1)}), bf16[512,4,512]{2,0,1:T(8,128)(2,1)}, u32[]{:S(2)}, u32[]{:S(2)}) async-start(bf16[512,4,512]{2,0,1:T(8,128)(2,1)} %bitcast.62), calls=%async_computation | async-start | bytes 4194304 | tf_op jit(solution)/shard_map/all_to_all | solution.py:207
  83.4 0.0 all-reduce.3.cloned.1.call-start
  83.4 0.1 compare_reduce_fusion
  83.6 2.3 collective-permute-start.4
  85.9 1.3 collective-permute-start.5
  87.1 0.1 and_bitcast_fusion
  87.3 0.1 fusion
  87.3 1.3 collective-permute-start
  88.6 1.5 pick_vertical.2
  90.1 1.5 pick_vertical.3
  91.7 0.1 add_select_fusion
  91.8 0.1 copy.51
  91.9 1.3 broadcast_in_dim.29
  93.2 1.5 slice.162.bias_ref
  94.7 63.8 %all-reduce.3.cloned.1.call-done = (bf16[1280,256]{1,0:T(8,128)(2,1)}, bf16[1280,256]{1,0:T(8,128)(2,1)}) async-done(((bf16[1280,256]{1,0:T(8,128)(2,1)}, bf16[1280,256]{1,0:T(8,128)(2,1)}), (bf16[1280,256]{1,0:T(8,128)(2,1)}, bf16[1280,256]{1,0:T(8,128)(2,1)})) %all-reduce.3.cloned.1.call-update) | async-done | bytes 1310736 | tf_op jit(solution)/shard_map/psum | solution.py:242
  158.5 1.1 copy-done.2
  159.6 48.7 %attend.3 = bf16[2048,512]{1,0:T(8,128)(2,1)} custom-call(s32[4,8]{1,0:T(4,128)S(1)} %get-tuple-element.33.slash_ref, s32[1]{0:T(128)} %bitcast.odd_ref, bf16[2048,512]{1,0:T(8,128)(2,1)} %bitcast.12.q_ref, bf16[2048,256]{1,0:T(8,128)(2,1)} %collective-permute-done.3.two_ref, bf16[2048,256]{1,0:T(8,128)(2,1)} %collective-permute-done.4.low_ref, ...), custom_call_target="tpu_custom_call" | custom-call | flops 3758096384 | bytes 58720256 | tf_op jit(solution)/shard_map/attend/pallas_call | solution.py:159
  208.3 4.6 %all-to-all-start.5 = ((bf16[4,512,512]{2,1,0:T(8,128)(2,1)}), bf16[4,512,512]{2,1,0:T(8,128)(2,1)}, u32[]{:S(2)}, u32[]{:S(2)}) async-start(bf16[4,512,512]{2,1,0:T(8,128)(2,1)} %bitcast.66), calls=%async_computation.5 | async-start | bytes 4194304 | tf_op jit(solution)/shard_map/all_to_all | solution.py:252
  212.9 1.4 collective-permute-start.1
  214.2 1.3 collective-permute-start.2
  215.5 0.1 copy.46
  215.7 1.3 broadcast_in_dim.28
  217.0 1.5 slice.144.bias_ref
  218.5 0.7 collective-permute-done.2.high_ref
  219.1 48.5 %attend.2 = bf16[2048,512]{1,0:T(8,128)(2,1)} custom-call(s32[4,8]{1,0:T(4,128)S(1)} %get-tuple-element.34.slash_ref, s32[1]{0:T(128)} %bitcast.odd_ref, bf16[2048,512]{1,0:T(8,128)(2,1)} %bitcast.2.q_ref, bf16[2048,256]{1,0:T(8,128)(2,1)} %collective-permute-done.two_ref, bf16[2048,256]{1,0:T(8,128)(2,1)S(1)} %collective-permute-done.1.low_ref, ...), custom_call_target="tpu_custom_call" | custom-call | flops 3758096384 | bytes 58720256 | tf_op jit(solution)/shard_map/attend/pallas_call | solution.py:159
  267.7 4.4 %all-to-all-start.2 = ((bf16[4,512,512]{2,1,0:T(8,128)(2,1)}), bf16[4,512,512]{2,1,0:T(8,128)(2,1)}, u32[]{:S(2)}, u32[]{:S(2)}) async-start(bf16[4,512,512]{2,1,0:T(8,128)(2,1)} %bitcast.67), calls=%async_computation.2 | async-start | bytes 4194304 | tf_op jit(solution)/shard_map/all_to_all | solution.py:252
  272.1 1.8 copy.59
  273.9 23.7 %all-to-all-done.2 = bf16[4,512,512]{2,1,0:T(8,128)(2,1)} async-done(((bf16[4,512,512]{2,1,0:T(8,128)(2,1)}), bf16[4,512,512]{2,1,0:T(8,128)(2,1)}, u32[]{:S(2)}, u32[]{:S(2)}) %all-to-all-start.2) | async-done | bytes 2097184 | tf_op jit(solution)/shard_map/all_to_all | solution.py:252
  297.7 1.9 copy.58
  299.7 0.1 slice_dynamic-update-slice_fusion.3
  299.8 0.1 slice_dynamic-update-slice_fusion.1
  299.9 2.0 copy-done.3
  301.9 0.8 slice_dynamic-update-slice_fusion
  (26 shorter events, 0.3 us)
Async XLA Ops:
  6.5 49.9 %copy-start = (s32[32,8]{0,1:T(8,128)S(1)}, s32[32,8]{0,1:T(8,128)}, u32[]{:S(2)}) copy-start(s32[32,8]{0,1:T(8,128)} %param.9) | copy-start | bytes 3076
  16.1 17.4 %all-to-all-start.1 = ((bf16[512,4,256]{2,0,1:T(8,128)(2,1)}), bf16[512,4,256]{2,0,1:T(8,128)(2,1)S(1)}, u32[]{:S(2)}, u32[]{:S(2)}) async-start(bf16[512,4,256]{2,0,1:T(8,128)(2,1)} %bitcast.45), calls=%async_computation.1 | async-start | bytes 2097152 | tf_op jit(solution)/shard_map/all_to_all | solution.py:207
  33.5 16.6 %all-to-all-start.4 = ((bf16[512,4,256]{2,0,1:T(8,128)(2,1)}), bf16[512,4,256]{2,0,1:T(8,128)(2,1)S(1)}, u32[]{:S(2)}, u32[]{:S(2)}) async-start(bf16[512,4,256]{2,0,1:T(8,128)(2,1)} %bitcast.44), calls=%async_computation.4 | async-start | bytes 2097152 | tf_op jit(solution)/shard_map/all_to_all | solution.py:207
  41.3 14.6 %copy-start.4 = (s32[32,5]{0,1:T(8,128)S(1)}, s32[32,5]{0,1:T(8,128)}, u32[]{:S(2)}) copy-start(s32[32,5]{0,1:T(8,128)} %param.8) | copy-start | bytes 1924
  50.1 28.9 %all-to-all-start.3 = ((bf16[512,4,512]{2,0,1:T(8,128)(2,1)}), bf16[512,4,512]{2,0,1:T(8,128)(2,1)}, u32[]{:S(2)}, u32[]{:S(2)}) async-start(bf16[512,4,512]{2,0,1:T(8,128)(2,1)} %bitcast.63), calls=%async_computation.3 | async-start | bytes 4194304 | tf_op jit(solution)/shard_map/all_to_all | solution.py:207
  54.6 31.3 %collective-permute-start.3 = (bf16[2048,256]{1,0:T(8,128)(2,1)S(1)}, bf16[2048,256]{1,0:T(8,128)(2,1)}, u32[]{:S(2)}, u32[]{:S(2)}) collective-permute-start(bf16[2048,256]{1,0:T(8,128)(2,1)S(1)} %bitcast.50), channel_id=1, source_target_pairs={{0,2},{1,3},{2,4},{3,5},{4,6},{5,7},{8,10},{9,11},{10,12},{11,13},... | collective-permute-start | bytes 3145736 | tf_op jit(solution)/shard_map/ppermute | solution.py:22
  78.9 129.3 %all-to-all-start = ((bf16[512,4,512]{2,0,1:T(8,128)(2,1)}), bf16[512,4,512]{2,0,1:T(8,128)(2,1)}, u32[]{:S(2)}, u32[]{:S(2)}) async-start(bf16[512,4,512]{2,0,1:T(8,128)(2,1)} %bitcast.62), calls=%async_computation | async-start | bytes 4194304 | tf_op jit(solution)/shard_map/all_to_all | solution.py:207
  83.4 75.1 %all-reduce.3.cloned.1.call-start = ((), (), s32[]{:S(2)}) async-start(), calls=%async_computation.6 | async-start | bytes 2621440 | tf_op jit(solution)/shard_map/psum | solution.py:242
  83.6 74.9 %collective-permute-start.4 = (bf16[2048,256]{1,0:T(8,128)(2,1)S(1)}, bf16[2048,256]{1,0:T(8,128)(2,1)}, u32[]{:S(2)}, u32[]{:S(2)}) collective-permute-start(bf16[2048,256]{1,0:T(8,128)(2,1)S(1)} %bitcast.51), channel_id=1, source_target_pairs={{0,1},{2,3},{4,5},{6,7},{8,9},{10,11},{12,13},{14,15},{16,17},{18,... | collective-permute-start | bytes 3145736 | tf_op jit(solution)/shard_map/ppermute | solution.py:243
  85.9 72.6 %collective-permute-start.5 = (bf16[2048,256]{1,0:T(8,128)(2,1)}, bf16[2048,256]{1,0:T(8,128)(2,1)}, u32[]{:S(2)}, u32[]{:S(2)}) collective-permute-start(bf16[2048,256]{1,0:T(8,128)(2,1)} %collective-permute-done.3.two_ref), channel_id=1, source_target_pairs={{1,0},{3,2},{5,4},{7,6},{9,8},{11,10},{13,12},{15,14},{17,16},{19,... | collective-permute-start | bytes 3145736 | tf_op jit(solution)/shard_map/ppermute | solution.py:247
  87.3 126.9 %collective-permute-start = (bf16[2048,256]{1,0:T(8,128)(2,1)S(1)}, bf16[2048,256]{1,0:T(8,128)(2,1)}, u32[]{:S(2)}, u32[]{:S(2)}) collective-permute-start(bf16[2048,256]{1,0:T(8,128)(2,1)S(1)} %bitcast.46), channel_id=1, source_target_pairs={{0,2},{1,3},{2,4},{3,5},{4,6},{5,7},{8,10},{9,11},{10,12},{11,13},... | collective-permute-start | bytes 3145736 | tf_op jit(solution)/shard_map/ppermute | solution.py:22
  158.5 1.1 copy-start.2
  208.3 10.9 %copy-start.1 = (bf16[1280,256]{1,0:T(8,128)(2,1)S(1)}, bf16[1280,256]{1,0:T(8,128)(2,1)}, u32[]{:S(2)}) copy-start(bf16[1280,256]{1,0:T(8,128)(2,1)} %get-tuple-element.5.vert_ref) | copy-start | bytes 1966084
  208.3 59.4 %all-to-all-start.5 = ((bf16[4,512,512]{2,1,0:T(8,128)(2,1)}), bf16[4,512,512]{2,1,0:T(8,128)(2,1)}, u32[]{:S(2)}, u32[]{:S(2)}) async-start(bf16[4,512,512]{2,1,0:T(8,128)(2,1)} %bitcast.66), calls=%async_computation.5 | async-start | bytes 4194304 | tf_op jit(solution)/shard_map/all_to_all | solution.py:252
  212.9 5.6 %collective-permute-start.1 = (bf16[2048,256]{1,0:T(8,128)(2,1)S(1)}, bf16[2048,256]{1,0:T(8,128)(2,1)S(1)}, u32[]{:S(2)}, u32[]{:S(2)}) collective-permute-start(bf16[2048,256]{1,0:T(8,128)(2,1)S(1)} %bitcast.48), channel_id=1, source_target_pairs={{0,1},{2,3},{4,5},{6,7},{8,9},{10,11},{12,13},{14,15},{16,17},{18,... | collective-permute-start | bytes 3145736 | tf_op jit(solution)/shard_map/ppermute | solution.py:243
  214.2 4.9 %collective-permute-start.2 = (bf16[2048,256]{1,0:T(8,128)(2,1)}, bf16[2048,256]{1,0:T(8,128)(2,1)}, u32[]{:S(2)}, u32[]{:S(2)}) collective-permute-start(bf16[2048,256]{1,0:T(8,128)(2,1)} %collective-permute-done.two_ref), channel_id=1, source_target_pairs={{1,0},{3,2},{5,4},{7,6},{9,8},{11,10},{13,12},{15,14},{17,16},{19,... | collective-permute-start | bytes 3145736 | tf_op jit(solution)/shard_map/ppermute | solution.py:247
  267.7 30.0 %all-to-all-start.2 = ((bf16[4,512,512]{2,1,0:T(8,128)(2,1)}), bf16[4,512,512]{2,1,0:T(8,128)(2,1)}, u32[]{:S(2)}, u32[]{:S(2)}) async-start(bf16[4,512,512]{2,1,0:T(8,128)(2,1)} %bitcast.67), calls=%async_computation.2 | async-start | bytes 4194304 | tf_op jit(solution)/shard_map/all_to_all | solution.py:252
  299.9 2.0 copy-start.3
Sparse Core Ops, SparseCore 0:
  91.8 66.6 all-reduce.2

commit v3 on v2

--- a/solution.py
+++ b/solution.py
@@ -22,22 +22,28 @@
     return lax.ppermute(value, axis, [(source, source + steps) for source in range(leading, last)])
 
 
-def pick_kernel(vert_count, offset_ref, kv_ref, out_ref):
+def pick_kernel(group, kv_heads, vert_count, offset_ref, kv_ref, out_ref):
     blocks = kv_ref.shape[0] // BLK
-    for slot in range(out_ref.shape[0] // BLK):
-        offset = offset_ref[slot]
-        inside = jnp.logical_and(offset >= 0, offset < blocks)
-        start = pl.multiple_of(jnp.clip(offset, 0, blocks - 1) * BLK, BLK)
-        piece = kv_ref[pl.ds(start, BLK), :]
-        out_ref[slot * BLK : (slot + 1) * BLK, :] = jnp.where(
-            inside, piece, jnp.zeros_like(piece)
-        )
-
-
-def pick_vertical(kv_local, offsets):
+    q_heads = out_ref.shape[0] // (vert_count * BLK)
+    for head in range(q_heads):
+        k_col = (head // group) * HD
+        v_col = (kv_heads + head // group) * HD
+        for slot in range(vert_count):
+            offset = offset_ref[head * vert_count + slot]
+            inside = jnp.logical_and(offset >= 0, offset < blocks)
+            start = pl.multiple_of(jnp.clip(offset, 0, blocks - 1) * BLK, BLK)
+            row = (head * vert_count + slot) * BLK
+            for place, col in ((0, k_col), (HD, v_col)):
+                piece = kv_ref[pl.ds(start, BLK), col : col + HD]
+                out_ref[row : row + BLK, place : place + HD] = jnp.where(
+                    inside, piece, jnp.zeros_like(piece)
+                )
+
+
+def pick_vertical(kv_local, offsets, group, kv_heads):
     q_heads, vert_count = offsets.shape
     return pl.pallas_call(
-        functools.partial(pick_kernel, vert_count),
+        functools.partial(pick_kernel, group, kv_heads, vert_count),
         out_shape=jax.ShapeDtypeStruct((q_heads * vert_count * BLK, 2 * HD), kv_local.dtype),
         in_specs=[
             pl.BlockSpec(memory_space=pltpu.SMEM),
@@ -50,6 +56,8 @@
 
 
 def attend_kernel(
+    group,
+    kv_heads,
     slash_ref,
     odd_ref,
     q_ref,
@@ -60,7 +68,8 @@
     vert_ref,
     bias_ref,
     out_ref,
-    window_ref,
+    key_ref,
+    value_ref,
 ):
     head = pl.program_id(0)
     slash_count = slash_ref.shape[1]
@@ -68,19 +77,38 @@
     blocks = rows // BLK
     front = 2 * blocks
 
-    @pl.when(head == 0)
-    def _():
-        window_ref[:rows, :] = two_ref[...]
-        window_ref[2 * rows :, :] = own_ref[...]
-
-        @pl.when(odd_ref[0] == 1)
+    def load_run(run, ref, kv):
+        first = run * rows
+        value_ref[first : first + rows, :] = ref[:, (kv_heads + kv) * HD : (kv_heads + kv + 1) * HD]
+
+        def turn(block, carry):
+            piece = ref[pl.ds(pl.multiple_of(block * BLK, BLK), BLK), kv * HD : (kv + 1) * HD]
+            key_ref[run * blocks + block] = jnp.concatenate([piece, piece], 0).T
+            return carry
+
+        lax.fori_loop(0, blocks, turn, 0, unroll=4)
+
+    for kv in range(kv_heads):
+
+        @pl.when(head == kv * group)
         def _():
-            window_ref[rows : 2 * rows, :] = low_ref[...]
-
-        @pl.when(odd_ref[0] == 0)
+            load_run(0, two_ref, kv)
+            load_run(2, own_ref, kv)
+
+        @pl.when(jnp.logical_and(head == kv * group, odd_ref[0] == 1))
         def _():
-            window_ref[rows : 2 * rows, :] = high_ref[...]
-
+            load_run(1, low_ref, kv)
+
+        @pl.when(jnp.logical_and(head == kv * group, odd_ref[0] == 0))
+        def _():
+            load_run(1, high_ref, kv)
+
+    left = lax.broadcasted_iota(jnp.int32, (HD, 2 * BLK), 1) < BLK
+    if (1 + slash_ref.shape[1]) % 2:
+        first_vert = vert_ref[:BLK, :HD]
+        lead_keys = [jnp.concatenate([first_vert, first_vert], 0).T]
+    else:
+        lead_keys = []
     scale = HD ** (-0.5) * math.log2(math.e)
     row_ids = lax.broadcasted_iota(jnp.int32, (BLK, 2 * BLK), 0)
     col_ids = lax.broadcasted_iota(jnp.int32, (BLK, 2 * BLK), 1)
@@ -105,16 +133,17 @@
             row = pl.multiple_of(block * BLK, BLK)
             starts = [pl.multiple_of((front + block - offset) * BLK, BLK) for offset in offsets]
 
-            def gathered(first):
-                pieces = [window_ref[pl.ds(start, BLK), first : first + HD] for start in starts]
-                if lead:
-                    pieces.append(vert_ref[:lead, first : first + HD])
-                return jnp.concatenate(pieces, 0)
-
-            scores = lax.dot_general(
+            halves = [key_ref[front + block - offset] for offset in offsets] + lead_keys
+            keys = [
+                jnp.where(left, halves[pair], halves[pair + 1])
+                for pair in range(0, len(halves), 2)
+            ]
+            values = [value_ref[pl.ds(start, BLK), :] for start in starts]
+            if lead:
+                values.append(vert_ref[:lead, HD:])
+            scores = jnp.dot(
                 q_ref[pl.ds(row, BLK), :],
-                gathered(0),
-                (((1,), (1,)), ((), ())),
+                jnp.concatenate(keys, 1),
                 preferred_element_type=jnp.float32,
             )
             scores = scores * scale + bias_ref[0, pl.ds(block, 1), :split]
@@ -134,7 +163,9 @@
             shared_weights.append(vert_weights.astype(jnp.bfloat16))
             sums.append(
                 jnp.dot(
-                    weights.astype(jnp.bfloat16), gathered(HD), preferred_element_type=jnp.float32
+                    weights.astype(jnp.bfloat16),
+                    jnp.concatenate(values, 0),
+                    preferred_element_type=jnp.float32,
                 )
             )
         summed = jnp.dot(
@@ -151,13 +182,13 @@
     lax.fori_loop(0, blocks // together, one_group, 0, unroll=2)
 
 
-def attend(queries, two_back, low, high, own, odd, vertical, slash, bias):
+def attend(queries, two_back, low, high, own, odd, vertical, slash, bias, group, kv_heads):
     rows = queries.shape[0]
     q_heads, blocks, width = bias.shape
     vert_rows = vertical.shape[0] // q_heads
-    whole = pl.BlockSpec((rows, 2 * HD), lambda h, s, o: (0, 0))
+    whole = pl.BlockSpec(own.shape, lambda h, s, o: (0, 0))
     return pl.pallas_call(
-        attend_kernel,
+        functools.partial(attend_kernel, group, kv_heads),
         out_shape=jax.ShapeDtypeStruct((rows, q_heads * HD), queries.dtype),
         grid_spec=pltpu.PrefetchScalarGridSpec(
             num_scalar_prefetch=2,
@@ -172,7 +203,10 @@
                 pl.BlockSpec((1, blocks, width), lambda h, s, o: (h, 0, 0)),
             ],
             out_specs=pl.BlockSpec((rows, HD), lambda h, s, o: (0, h)),
-            scratch_shapes=[pltpu.VMEM((3 * rows, 2 * HD), queries.dtype)],
+            scratch_shapes=[
+                pltpu.VMEM((3 * blocks, HD, 2 * BLK), queries.dtype),
+                pltpu.VMEM((3 * rows, HD), queries.dtype),
+            ],
         ),
         compiler_params=pltpu.CompilerParams(
             dimension_semantics=("arbitrary",), vmem_limit_bytes=VMEM_LIMIT
@@ -197,30 +231,23 @@
     kv_heads = KVH * copies // head_count
     group = q_heads // kv_heads
 
-    wide = group * HD
-
-    def columns(array, first, width):
-        return lax.slice_in_dim(array, first, first + width, axis=1)
-
-    def to_heads(pieces):
-        flat = jnp.concatenate(pieces, axis=1)
-        return lax.all_to_all(flat, "head", split_axis=1, concat_axis=0, tiled=True)
-
-    own = [
-        to_heads(
-            [
-                columns(states, (peer * kv_heads + kv) // copies * HD, HD)
-                for peer in range(head_count)
-                for states in (key_states, value_states)
-            ]
-        )
-        for kv in range(kv_heads)
-    ]
-    row_count = own[0].shape[0]
+    def by_head(states):
+        split = states.reshape(rows_in, KVH, HD)
+        if copies > 1:
+            split = jnp.repeat(split, copies, axis=1)
+        return split.reshape(rows_in, head_count, kv_heads * HD)
+
+    kv_pair = jnp.concatenate([by_head(key_states), by_head(value_states)], axis=2)
+    kv_pair = kv_pair.reshape(rows_in, head_count * 2 * kv_heads * HD)
+    kv_local = lax.all_to_all(kv_pair, "head", split_axis=1, concat_axis=0, tiled=True)
+    row_count = kv_local.shape[0]
     blocks = row_count // BLK
     vert_mine = lax.dynamic_slice_in_dim(vertical_blocks, head_index * q_heads, q_heads, 0)
     slash_mine = lax.dynamic_slice_in_dim(slash_offsets, head_index * q_heads, q_heads, 0)
     first_block = block_index * blocks
+    own_vertical = pick_vertical(kv_local, vert_mine - first_block, group, kv_heads)
+    own_vertical, queries, vert_mine = lax.optimization_barrier((own_vertical, queries, vert_mine))
+    vertical = lax.psum(own_vertical, "qblk")
     odd = lax.rem(block_index, 2).astype(jnp.int32).reshape(1)
 
     block_ids = first_block + jnp.arange(blocks, dtype=jnp.int32)
@@ -235,25 +262,24 @@
 
     upward = [(run, run + 1) for run in range(0, run_count - 1, 2)]
     downward = [(run + 1, run) for run in range(0, run_count - 1, 2)]
-    returned = []
-    for kv in range(kv_heads):
-        heads = slice(kv * group, (kv + 1) * group)
-        two_back = from_behind(own[kv], "qblk", 2)
-        vertical = lax.psum(pick_vertical(own[kv], vert_mine[heads] - first_block), "qblk")
-        low = lax.ppermute(own[kv], "qblk", upward)
-        q_local = to_heads(
-            [columns(queries, (peer * kv_heads + kv) * wide, wide) for peer in range(head_count)]
-        )
-        high = lax.ppermute(two_back, "qblk", downward)
-        attended = attend(
-            q_local, two_back, low, high, own[kv], odd, vertical, slash_mine[heads], bias[heads]
-        )
-        returned.append(
-            lax.all_to_all(attended, "head", split_axis=0, concat_axis=1, tiled=True)
-        )
-    return jnp.concatenate(
-        [columns(part, peer * wide, wide) for peer in range(head_count) for part in returned], 1
+    two_back = from_behind(kv_local, "qblk", 2)
+    low = lax.ppermute(kv_local, "qblk", upward)
+    high = lax.ppermute(two_back, "qblk", downward)
+    q_local = lax.all_to_all(queries, "head", split_axis=1, concat_axis=0, tiled=True)
+    attended = attend(
+        q_local,
+        two_back,
+        low,
+        high,
+        kv_local,
+        odd,
+        vertical,
+        slash_mine,
+        bias,
+        group,
+        kv_heads,
     )
+    return lax.all_to_all(attended, "head", split_axis=0, concat_axis=1, tiled=True)
 
 
 def solution(mesh):

time: 315 us -> 302 us (0.959)
  blocking collectives: 0 us -> 80 us
  waiting for transfers between devices: 127 us -> 87.6 us
  starting transfers between devices: 34 us -> 10.1 us
  local copies, waits for them, and re-layouts: 32.4 us -> 14.7 us
  Pallas kernels: 100 us -> 92.2 us
    all_to_all x0 -> x2, blocking collectives: none -> 80 us  [the longest x1 51.1 us: per_device(): lax.all_to_all(attended, 'head', split_axis=0, concat_axis=1, tiled=True)]
    all_to_all x6 -> x1, waiting for transfers between devices: 62.7 us -> 0.01 us  [per_device(): lax.all_to_all(queries, 'head', split_axis=1, concat_axis=0, tiled=True)]
    ppermute x2 -> x1, waiting for transfers between devices: 0.01 us -> 31.9 us  [from_behind(): lax.ppermute(value, axis, [(source, source + steps) for source in range(l...]
    all_to_all x6 -> x1, starting transfers between devices: 25.2 us -> 4.84 us  [per_device(): lax.all_to_all(queries, 'head', split_axis=1, concat_axis=0, tiled=True)]
    unnamed x25 -> x9, local copies, waits for them, and re-layouts: 10.9 us -> 1.4 us
    psum x1, waiting for transfers between devices: 63.8 us -> 55.7 us  [per_device(): vertical = lax.psum(own_vertical, 'qblk')]
    pallas_call x4 -> x2, Pallas kernels: 100 us -> 92.2 us  [the longest x1 90.2 us: attend(): pl.pallas_call(functools.partial(attend_kernel, group, kv_heads), out_sha...]
    slice x7 -> x0, local copies, waits for them, and re-layouts: 5.9 us -> none  [the longest x5 3.26 us: per_device(): bias[heads]]
  transfers between devices with their start and end apart: 13 -> 5, of which waited for: 6 -> 2; matrix products, arithmetic and copies ran while one was open for 6% -> 3% of each run, Pallas kernels for 32% -> 1%
where the time goes in v3:
time: 302 us; the launch traced here: 299 us
  Pallas kernels  92.2 us (31%)
  waiting for transfers between devices  87.6 us (29%)
  blocking collectives  80 us (26%)
  local copies, waits for them, and re-layouts  14.7 us (5%)
  between operations  13.5 us (4%)
  starting transfers between devices  10.1 us (3%)
    pallas_call x1, Pallas kernels, attend(): pl.pallas_call(functools.partial(attend_kernel, group, kv_heads), out_sha...  90.2 us
    psum x1, waiting for transfers between devices, per_device(): vertical = lax.psum(own_vertical, 'qblk')  55.7 us
    all_to_all x1, blocking collectives, per_device(): lax.all_to_all(attended, 'head', split_axis=0, concat_axis=1, tiled=True)  51.1 us
    ppermute x1, waiting for transfers between devices, from_behind(): lax.ppermute(value, axis, [(source, source + steps) for source in range(l...  31.9 us
    all_to_all x1, blocking collectives, per_device(): lax.all_to_all(kv_pair, 'head', split_axis=1, concat_axis=0, tiled=True)  28.9 us
  transfers between devices with their start and end apart: 5, of which 2 were waited for; matrix products, arithmetic and copies ran while one was open for 3% of the time, Pallas kernels for 1%

profile of v3, /device:TPU:24, one launch (start us, length us, event | category | flops | bytes accessed | tf_op | source)
XLA Modules:
  0.0 298.9 jit_solution(2473516587750311714)
XLA Ops:
  6.5 0.0 copy-start
  6.5 1.7 copy_bitcast_fusion.1
  8.2 0.2 pad_maximum_fusion
  8.4 0.0 copy-start.3
  8.4 28.9 %all_to_all.54 = bf16[512,4,512]{2,0,1:T(8,128)(2,1)S(1)} all-to-all(bf16[512,4,512]{2,0,1:T(8,128)(2,1)S(1)} %pad_maximum_fusion), channel_id=1, replica_groups=mesh['head'=4,'qblk'=8] {'head'}, dimensions={1} | all-to-all | bytes 4194304 | tf_op jit(solution)/shard_map/all_to_all | solution.py:242
  37.3 0.0 copy-start.1
  37.3 1.3 collective-permute-start
  38.6 0.0 copy-done.3
  38.6 0.1 broadcast_subtract_fusion.1
  38.7 0.1 copy.30
  38.8 0.1 reshape.45.offset_ref
  38.9 2.0 pick_vertical.1
  40.9 4.8 %copy.47 = bf16[64,4,8,1024]{3,2,0,1:T(8,128)(2,1)} copy(bf16[64,4,8,1024]{3,2,1,0:T(8,128)(2,1)} %bitcast.28) | data formatting | bytes 8388608 | tf_op jit(solution)/shard_map/all_to_all | solution.py:268
  45.7 4.8 %all-to-all-start.1 = ((bf16[512,4,1024]{2,0,1:T(8,128)(2,1)}), bf16[512,4,1024]{2,0,1:T(8,128)(2,1)}, u32[]{:S(2)}, u32[]{:S(2)}) async-start(bf16[512,4,1024]{2,0,1:T(8,128)(2,1)} %bitcast.26), calls=%async_computation.1 | async-start | bytes 8388608 | tf_op jit(solution)/shard_map/all_to_all | solution.py:268
  50.5 0.0 all-reduce.2.cloned.1.call-start
  50.6 0.0 copy-done.1
  50.6 2.7 collective-permute-start.1
  53.2 31.9 %collective-permute-done.two_ref = bf16[2048,512]{1,0:T(8,128)(2,1)} collective-permute-done((bf16[2048,512]{1,0:T(8,128)(2,1)S(1)}, bf16[2048,512]{1,0:T(8,128)(2,1)}, u32[]{:S(2)}, u32[]{:S(2)}) %collective-permute-start) | collective-permute-done | bytes 2097184 | tf_op jit(solution)/shard_map/ppermute | solution.py:22
  85.1 1.3 collective-permute-start.2
  86.4 0.0 copy-done
  86.4 0.1 constant_dynamic-slice_fusion.1
  86.5 0.1 copy.39.slash_ref
  86.6 0.1 subtract_compare_fusion
  86.7 0.1 copy.35
  86.8 0.0 all-reduce.2.cloned.1.call-update
  86.8 0.1 broadcast_subtract_fusion
  86.9 0.1 compare_reduce_fusion
  87.0 0.1 not_and_fusion
  87.1 0.1 add_select_fusion
  87.2 0.1 copy.37
  87.3 1.9 broadcast_in_dim.26
  89.3 2.0 reshape.46.bias_ref
  91.3 55.7 %all-reduce.2.cloned.1.call-done.vert_ref = bf16[2560,256]{1,0:T(8,128)(2,1)} async-done(((bf16[2560,256]{1,0:T(8,128)(2,1)}), bf16[2560,256]{1,0:T(8,128)(2,1)}) %all-reduce.2.cloned.1.call-update) | async-done | bytes 1310736 | tf_op jit(solution)/shard_map/psum | solution.py:250
  147.0 0.0 collective-permute-done.1.low_ref
  147.0 0.0 all-to-all-done.1
  147.0 0.0 collective-permute-done.2.high_ref
  147.0 0.0 copy-start.2
  147.0 1.3 copy-done.2
  148.3 90.2 %attend.1 = bf16[2048,1024]{1,0:T(8,128)(2,1)} custom-call(s32[8,8]{1,0:T(8,128)S(1)} %copy.39.slash_ref, s32[1]{0:T(128)} %bitcast.odd_ref, bf16[2048,1024]{1,0:T(8,128)(2,1)} %bitcast.4.q_ref, bf16[2048,512]{1,0:T(8,128)(2,1)} %collective-permute-done.two_ref, bf16[2048,512]{1,0:T(8,128)(2,1)} %collective-permute-done.1.low_ref, ...), custom_call_target="tpu_custom_call" | custom-call | flops 7516192768 | bytes 117440512 | tf_op jit(solution)/shard_map/attend/pallas_call | solution.py:190
  238.5 51.1 %all_to_all.55 = bf16[4,512,1024]{2,1,0:T(8,128)(2,1)S(1)} all-to-all(bf16[4,512,1024]{2,1,0:T(8,128)(2,1)} %bitcast.29), channel_id=1, replica_groups=mesh['head'=4,'qblk'=8] {'head'}, dimensions={0} | all-to-all | bytes 8388608 | tf_op jit(solution)/shard_map/all_to_all | solution.py:282
  289.6 2.5 copy.43
  (3 shorter events, 0.0 us)
Async XLA Ops:
  6.5 79.9 %copy-start = (s32[32,8]{0,1:T(8,128)S(1)}, s32[32,8]{0,1:T(8,128)}, u32[]{:S(2)}) copy-start(s32[32,8]{0,1:T(8,128)} %param.9) | copy-start | bytes 3076
  8.4 30.2 %copy-start.3 = (s32[32,5]{0,1:T(8,128)S(1)}, s32[32,5]{0,1:T(8,128)}, u32[]{:S(2)}) copy-start(s32[32,5]{0,1:T(8,128)} %param.8) | copy-start | bytes 1924
  37.3 13.3 %copy-start.1 = (bf16[512,4,512]{2,0,1:T(8,128)(2,1)}, bf16[512,4,512]{2,0,1:T(8,128)(2,1)S(1)}, u32[]{:S(2)}) copy-start(bf16[512,4,512]{2,0,1:T(8,128)(2,1)S(1)} %all_to_all.54) | copy-start | bytes 6291460
  37.3 47.8 %collective-permute-start = (bf16[2048,512]{1,0:T(8,128)(2,1)S(1)}, bf16[2048,512]{1,0:T(8,128)(2,1)}, u32[]{:S(2)}, u32[]{:S(2)}) collective-permute-start(bf16[2048,512]{1,0:T(8,128)(2,1)S(1)} %bitcast.22), channel_id=1, source_target_pairs={{0,2},{1,3},{2,4},{3,5},{4,6},{5,7},{8,10},{9,11},{10,12},{11,13},... | collective-permute-start | bytes 6291464 | tf_op jit(solution)/shard_map/ppermute | solution.py:22
  45.7 101.3 %all-to-all-start.1 = ((bf16[512,4,1024]{2,0,1:T(8,128)(2,1)}), bf16[512,4,1024]{2,0,1:T(8,128)(2,1)}, u32[]{:S(2)}, u32[]{:S(2)}) async-start(bf16[512,4,1024]{2,0,1:T(8,128)(2,1)} %bitcast.26), calls=%async_computation.1 | async-start | bytes 8388608 | tf_op jit(solution)/shard_map/all_to_all | solution.py:268
  50.5 96.5 %all-reduce.2.cloned.1.call-start = ((), (), s32[]{:S(2)}) async-start(), calls=%async_computation.3 | async-start | bytes 2621440 | tf_op jit(solution)/shard_map/psum | solution.py:250
  50.6 96.4 %collective-permute-start.1 = (bf16[2048,512]{1,0:T(8,128)(2,1)S(1)}, bf16[2048,512]{1,0:T(8,128)(2,1)}, u32[]{:S(2)}, u32[]{:S(2)}) collective-permute-start(bf16[2048,512]{1,0:T(8,128)(2,1)S(1)} %bitcast.24), channel_id=1, source_target_pairs={{0,1},{2,3},{4,5},{6,7},{8,9},{10,11},{12,13},{14,15},{16,17},{18,... | collective-permute-start | bytes 6291464 | tf_op jit(solution)/shard_map/ppermute | solution.py:266
  85.1 61.8 %collective-permute-start.2 = (bf16[2048,512]{1,0:T(8,128)(2,1)}, bf16[2048,512]{1,0:T(8,128)(2,1)}, u32[]{:S(2)}, u32[]{:S(2)}) collective-permute-start(bf16[2048,512]{1,0:T(8,128)(2,1)} %collective-permute-done.two_ref), channel_id=1, source_target_pairs={{1,0},{3,2},{5,4},{7,6},{9,8},{11,10},{13,12},{15,14},{17,16},{19,... | collective-permute-start | bytes 6291464 | tf_op jit(solution)/shard_map/ppermute | solution.py:267
  147.0 1.3 copy-start.2
Sparse Core Ops, SparseCore 0:
  86.9 60.0 all-reduce.1

commit v4 on v3

--- a/solution.py
+++ b/solution.py
@@ -53,6 +53,133 @@
         compiler_params=pltpu.CompilerParams(vmem_limit_bytes=VMEM_LIMIT),
         name="pick_vertical",
     )(offsets.reshape(-1), kv_local)
+
+
+def chain_kernel(
+    pieces,
+    own_ref,
+    out_ref,
+    total_ref,
+    inbox_ref,
+    carry_ref,
+    swap_sems,
+    down_sems,
+    arrive_sems,
+    give_sems,
+    take_sems,
+):
+    run = lax.axis_index("qblk")
+    runs = lax.axis_size("qblk")
+    core = lax.rem(run, 2)
+    partner = run + 1 - 2 * core
+    first = run < 2
+    last = run >= runs - 2
+    half = own_ref.shape[0] // 2
+    rows = half // pieces
+    mine = pl.multiple_of(core * half, BLK)
+    other = pl.multiple_of((1 - core) * half, BLK)
+
+    def send(src, dst, send_sem, recv_sem, target):
+        return pltpu.make_async_remote_copy(
+            src_ref=src,
+            dst_ref=dst,
+            send_sem=send_sem,
+            recv_sem=recv_sem,
+            device_id={"qblk": target},
+            device_id_type=pl.DeviceIdType.MESH,
+        )
+
+    barrier = pltpu.get_barrier_semaphore()
+    pl.semaphore_signal(
+        barrier, inc=1, device_id={"qblk": partner}, device_id_type=pl.DeviceIdType.MESH
+    )
+
+    @pl.when(jnp.logical_not(first))
+    def _():
+        pl.semaphore_signal(
+            barrier, inc=1, device_id={"qblk": run - 2}, device_id_type=pl.DeviceIdType.MESH
+        )
+
+    @pl.when(jnp.logical_not(last))
+    def _():
+        pl.semaphore_signal(
+            barrier, inc=1, device_id={"qblk": run + 2}, device_id_type=pl.DeviceIdType.MESH
+        )
+
+    pl.semaphore_wait(barrier, 1 + jnp.where(first, 0, 1) + jnp.where(last, 0, 1))
+
+    swap = send(own_ref.at[pl.ds(other, half)], inbox_ref, swap_sems.at[0], swap_sems.at[1], partner)
+    swap.start()
+    swap.wait()
+
+    def passed(piece):
+        part = total_ref.at[pl.ds(pl.multiple_of(mine + piece * rows, 16), rows)]
+        return send(
+            part, carry_ref.at[pl.ds(piece * rows, rows)], down_sems.at[piece],
+            arrive_sems.at[piece], run + 2,
+        )
+
+    def given(piece):
+        part = total_ref.at[pl.ds(pl.multiple_of(mine + piece * rows, 16), rows)]
+        return send(part, part, give_sems.at[piece], take_sems.at[piece], partner)
+
+    def taken(piece):
+        part = total_ref.at[pl.ds(pl.multiple_of(other + piece * rows, 16), rows)]
+        return send(part, part, give_sems.at[piece], take_sems.at[piece], partner)
+
+    for piece in range(pieces):
+        span = pl.ds(piece * rows, rows)
+        place = pl.ds(pl.multiple_of(mine + piece * rows, 16), rows)
+        total_ref[place, :] = own_ref[place, :] + inbox_ref[span, :]
+
+        @pl.when(jnp.logical_not(first))
+        def _():
+            passed(piece).wait_recv()
+            total_ref[place, :] = total_ref[place, :] + carry_ref[span, :]
+
+        @pl.when(jnp.logical_not(last))
+        def _():
+            passed(piece).start()
+
+        given(piece).start()
+
+    for piece in range(pieces):
+        taken(piece).wait_recv()
+        given(piece).wait_send()
+
+        @pl.when(jnp.logical_not(last))
+        def _():
+            passed(piece).wait_send()
+
+    out_ref[...] = total_ref[...]
+
+
+def sum_up_to_here(own):
+    rows, width = own.shape
+    pieces = 4
+    if lax.axis_size("qblk") % 2 or rows % (2 * pieces * 16):
+        return lax.psum(own, "qblk")
+    return pl.pallas_call(
+        functools.partial(chain_kernel, pieces),
+        out_shape=jax.ShapeDtypeStruct(own.shape, own.dtype),
+        in_specs=[pl.BlockSpec(memory_space=pltpu.VMEM)],
+        out_specs=pl.BlockSpec(memory_space=pltpu.VMEM),
+        scratch_shapes=[
+            pltpu.VMEM((rows, width), own.dtype),
+            pltpu.VMEM((rows // 2, width), own.dtype),
+            pltpu.VMEM((rows // 2, width), own.dtype),
+            pltpu.SemaphoreType.DMA((2,)),
+            pltpu.SemaphoreType.DMA((pieces,)),
+            pltpu.SemaphoreType.DMA((pieces,)),
+            pltpu.SemaphoreType.DMA((pieces,)),
+            pltpu.SemaphoreType.DMA((pieces,)),
+        ],
+        compiler_params=pltpu.CompilerParams(
+            collective_id=0, has_side_effects=True, vmem_limit_bytes=VMEM_LIMIT // 2
+        ),
+        cost_estimate=pl.CostEstimate(flops=0, bytes_accessed=64 * own.size, transcendentals=0),
+        name="sum_up_to_here",
+    )(own)
 
 
 def attend_kernel(
@@ -246,8 +373,8 @@
     slash_mine = lax.dynamic_slice_in_dim(slash_offsets, head_index * q_heads, q_heads, 0)
     first_block = block_index * blocks
     own_vertical = pick_vertical(kv_local, vert_mine - first_block, group, kv_heads)
-    own_vertical, queries, vert_mine = lax.optimization_barrier((own_vertical, queries, vert_mine))
-    vertical = lax.psum(own_vertical, "qblk")
+    own_vertical, vert_mine = lax.optimization_barrier((own_vertical, vert_mine))
+    vertical = sum_up_to_here(own_vertical)
     odd = lax.rem(block_index, 2).astype(jnp.int32).reshape(1)
 
     block_ids = first_block + jnp.arange(blocks, dtype=jnp.int32)

time: 302 us -> 266 us (0.88)
  waiting for transfers between devices: 87.6 us -> 36.4 us
  Pallas kernels: 92.2 us -> 122 us
  between operations: 13.5 us -> 0.14 us
    psum x1 -> x0, waiting for transfers between devices: 55.7 us -> none  [per_device(): vertical = lax.psum(own_vertical, 'qblk')]
    pallas_call x0 -> x1, Pallas kernels: none -> 30.5 us  [sum_up_to_here(): pl.pallas_call(functools.partial(chain_kernel, pieces), out_shape=jax.Sha...]
    ppermute x1, waiting for transfers between devices: 31.9 us -> 36.4 us  [from_behind(): lax.ppermute(value, axis, [(source, source + steps) for source in range(l...]
  transfers between devices with their start and end apart: 5 -> 4, of which waited for: 2 -> 1; matrix products, arithmetic and copies ran while one was open for 3% -> 4% of each run, Pallas kernels for 1% -> 12%
where the time goes in v4:
time: 266 us; the launch traced here: 265 us
  Pallas kernels  122 us (46%)
  blocking collectives  81.6 us (31%)
  waiting for transfers between devices  36.4 us (14%)
  local copies, waits for them, and re-layouts  13.8 us (5%)
  starting transfers between devices  10.2 us (4%)
    pallas_call x1, Pallas kernels, attend(): pl.pallas_call(functools.partial(attend_kernel, group, kv_heads), out_sha...  90.5 us
    all_to_all x1, blocking collectives, per_device(): lax.all_to_all(attended, 'head', split_axis=0, concat_axis=1, tiled=True)  52.4 us
    ppermute x1, waiting for transfers between devices, from_behind(): lax.ppermute(value, axis, [(source, source + steps) for source in range(l...  36.4 us
    pallas_call x1, Pallas kernels, sum_up_to_here(): pl.pallas_call(functools.partial(chain_kernel, pieces), out_shape=jax.Sha...  30.5 us
    all_to_all x1, blocking collectives, per_device(): lax.all_to_all(kv_pair, 'head', split_axis=1, concat_axis=0, tiled=True)  29.2 us
  transfers between devices with their start and end apart: 4, of which 1 were waited for; matrix products, arithmetic and copies ran while one was open for 4% of the time, Pallas kernels for 12%

profile of v4, /device:TPU:24, one launch (start us, length us, event | category | flops | bytes accessed | tf_op | source)
XLA Modules:
  0.0 265.4 jit_solution(13285820688452485485)
XLA Ops:
  0.0 0.0 copy-start
  0.0 1.7 copy_bitcast_fusion.1
  1.7 0.2 pad_maximum_fusion
  1.9 0.0 copy-start.3
  1.9 29.2 %all_to_all.54 = bf16[512,4,512]{2,0,1:T(8,128)(2,1)S(1)} all-to-all(bf16[512,4,512]{2,0,1:T(8,128)(2,1)S(1)} %pad_maximum_fusion), channel_id=1, replica_groups=mesh['head'=4,'qblk'=8] {'head'}, dimensions={1} | all-to-all | bytes 4194304 | tf_op jit(solution)/shard_map/all_to_all | solution.py:369
  31.0 0.0 copy-start.1
  31.0 1.3 collective-permute-start
  32.3 0.0 copy-done.3
  32.3 2.5 copy.47
  34.8 0.0 copy-start.4
  34.8 5.0 %all-to-all-start = ((bf16[512,4,1024]{2,0,1:T(8,128)(2,1)}), bf16[512,4,1024]{2,0,1:T(8,128)(2,1)}, u32[]{:S(2)}, u32[]{:S(2)}) async-start(bf16[512,4,1024]{2,0,1:T(8,128)(2,1)} %bitcast.26), calls=%async_computation | async-start | bytes 8388608 | tf_op jit(solution)/shard_map/all_to_all | solution.py:395
  39.8 2.6 collective-permute-start.1
  42.4 36.4 %collective-permute-done.two_ref = bf16[2048,512]{1,0:T(8,128)(2,1)} collective-permute-done((bf16[2048,512]{1,0:T(8,128)(2,1)S(1)}, bf16[2048,512]{1,0:T(8,128)(2,1)}, u32[]{:S(2)}, u32[]{:S(2)}) %collective-permute-start) | collective-permute-done | bytes 2097184 | tf_op jit(solution)/shard_map/ppermute | solution.py:22
  78.9 1.3 collective-permute-start.2
  80.2 0.0 copy-done
  80.2 0.1 constant_dynamic-slice_fusion.1
  80.2 0.1 copy.39.slash_ref
  80.3 0.0 copy-done.4
  80.3 0.1 broadcast_subtract_fusion.1
  80.4 0.1 copy.33
  80.5 0.1 reshape.45.offset_ref
  80.6 0.1 subtract_compare_fusion
  80.7 0.0 copy-done.1
  80.7 0.9 pick_vertical.1.own_ref
  81.6 30.5 %sum_up_to_here.1.vert_ref = bf16[2560,256]{1,0:T(8,128)(2,1)S(1)} custom-call(bf16[2560,256]{1,0:T(8,128)(2,1)S(1)} %pick_vertical.1.own_ref), custom_call_target="tpu_custom_call" | custom-call | bytes 41943040 | tf_op jit(solution)/shard_map/sum_up_to_here/pallas_call | solution.py:162
  112.2 0.1 copy.35
  112.3 0.1 broadcast_subtract_fusion
  112.3 0.1 compare_reduce_fusion
  112.5 0.1 not_and_fusion
  112.6 0.7 add_select_fusion
  113.3 0.9 copy.37
  114.2 1.9 broadcast_in_dim.26
  116.2 2.8 %reshape.46.bias_ref = f32[8,32,896]{2,1,0:T(8,128)} reshape(f32[8,32,14,64]{3,2,1,0:T(8,128)} %broadcast_in_dim.26) | data formatting | bytes 1835008 | tf_op jit(solution)/shard_map/reshape | solution.py:388
  118.9 0.0 all-to-all-done
  118.9 0.0 collective-permute-done.1.low_ref
  118.9 0.0 collective-permute-done.2.high_ref
  118.9 0.0 copy-start.2
  118.9 1.2 copy-done.2
  120.1 90.5 %attend.1 = bf16[2048,1024]{1,0:T(8,128)(2,1)} custom-call(s32[8,8]{1,0:T(8,128)S(1)} %copy.39.slash_ref, s32[1]{0:T(128)} %bitcast.odd_ref, bf16[2048,1024]{1,0:T(8,128)(2,1)} %bitcast.2.q_ref, bf16[2048,512]{1,0:T(8,128)(2,1)} %collective-permute-done.two_ref, bf16[2048,512]{1,0:T(8,128)(2,1)} %collective-permute-done.1.low_ref, ...), custom_call_target="tpu_custom_call" | custom-call | flops 7516192768 | bytes 117440512 | tf_op jit(solution)/shard_map/attend/pallas_call | solution.py:317
  210.6 52.4 %all_to_all.55 = bf16[4,512,1024]{2,1,0:T(8,128)(2,1)S(1)} all-to-all(bf16[4,512,1024]{2,1,0:T(8,128)(2,1)} %bitcast.29), channel_id=1, replica_groups=mesh['head'=4,'qblk'=8] {'head'}, dimensions={0} | all-to-all | bytes 8388608 | tf_op jit(solution)/shard_map/all_to_all | solution.py:409
  263.0 2.5 copy.43
  (3 shorter events, 0.0 us)
Async XLA Ops:
  0.0 80.2 %copy-start = (s32[32,8]{0,1:T(8,128)S(1)}, s32[32,8]{0,1:T(8,128)}, u32[]{:S(2)}) copy-start(s32[32,8]{0,1:T(8,128)} %param.9) | copy-start | bytes 3076
  1.9 30.5 %copy-start.3 = (bf16[512,4096]{1,0:T(8,128)(2,1)S(1)}, bf16[512,4096]{1,0:T(8,128)(2,1)}, u32[]{:S(2)}) copy-start(bf16[512,4096]{1,0:T(8,128)(2,1)} %param.5) | copy-start | bytes 12582916
  31.0 49.6 %copy-start.1 = (bf16[512,4,512]{2,0,1:T(8,128)(2,1)}, bf16[512,4,512]{2,0,1:T(8,128)(2,1)S(1)}, u32[]{:S(2)}) copy-start(bf16[512,4,512]{2,0,1:T(8,128)(2,1)S(1)} %all_to_all.54) | copy-start | bytes 6291460
  31.0 47.8 %collective-permute-start = (bf16[2048,512]{1,0:T(8,128)(2,1)S(1)}, bf16[2048,512]{1,0:T(8,128)(2,1)}, u32[]{:S(2)}, u32[]{:S(2)}) collective-permute-start(bf16[2048,512]{1,0:T(8,128)(2,1)S(1)} %bitcast.22), channel_id=1, source_target_pairs={{0,2},{1,3},{2,4},{3,5},{4,6},{5,7},{8,10},{9,11},{10,12},{11,13},... | collective-permute-start | bytes 6291464 | tf_op jit(solution)/shard_map/ppermute | solution.py:22
  34.8 45.5 %copy-start.4 = (s32[32,5]{0,1:T(8,128)S(1)}, s32[32,5]{0,1:T(8,128)}, u32[]{:S(2)}) copy-start(s32[32,5]{0,1:T(8,128)} %param.8) | copy-start | bytes 1924
  34.8 84.1 %all-to-all-start = ((bf16[512,4,1024]{2,0,1:T(8,128)(2,1)}), bf16[512,4,1024]{2,0,1:T(8,128)(2,1)}, u32[]{:S(2)}, u32[]{:S(2)}) async-start(bf16[512,4,1024]{2,0,1:T(8,128)(2,1)} %bitcast.26), calls=%async_computation | async-start | bytes 8388608 | tf_op jit(solution)/shard_map/all_to_all | solution.py:395
  39.8 79.1 %collective-permute-start.1 = (bf16[2048,512]{1,0:T(8,128)(2,1)S(1)}, bf16[2048,512]{1,0:T(8,128)(2,1)}, u32[]{:S(2)}, u32[]{:S(2)}) collective-permute-start(bf16[2048,512]{1,0:T(8,128)(2,1)S(1)} %bitcast.23), channel_id=1, source_target_pairs={{0,1},{2,3},{4,5},{6,7},{8,9},{10,11},{12,13},{14,15},{16,17},{18,... | collective-permute-start | bytes 6291464 | tf_op jit(solution)/shard_map/ppermute | solution.py:393
  78.9 40.1 %collective-permute-start.2 = (bf16[2048,512]{1,0:T(8,128)(2,1)}, bf16[2048,512]{1,0:T(8,128)(2,1)}, u32[]{:S(2)}, u32[]{:S(2)}) collective-permute-start(bf16[2048,512]{1,0:T(8,128)(2,1)} %collective-permute-done.two_ref), channel_id=1, source_target_pairs={{1,0},{3,2},{5,4},{7,6},{9,8},{11,10},{13,12},{15,14},{17,16},{19,... | collective-permute-start | bytes 6291464 | tf_op jit(solution)/shard_map/ppermute | solution.py:394
  118.9 1.2 copy-start.2

commit v5 on v4

--- a/solution.py
+++ b/solution.py
@@ -183,7 +183,7 @@
 
 
 def attend_kernel(
-    group,
+    kv,
     kv_heads,
     slash_ref,
     odd_ref,
@@ -215,20 +215,18 @@
 
         lax.fori_loop(0, blocks, turn, 0, unroll=4)
 
-    for kv in range(kv_heads):
-
-        @pl.when(head == kv * group)
-        def _():
-            load_run(0, two_ref, kv)
-            load_run(2, own_ref, kv)
-
-        @pl.when(jnp.logical_and(head == kv * group, odd_ref[0] == 1))
-        def _():
-            load_run(1, low_ref, kv)
-
-        @pl.when(jnp.logical_and(head == kv * group, odd_ref[0] == 0))
-        def _():
-            load_run(1, high_ref, kv)
+    @pl.when(head == 0)
+    def _():
+        load_run(0, two_ref, kv)
+        load_run(2, own_ref, kv)
+
+    @pl.when(jnp.logical_and(head == 0, odd_ref[0] == 1))
+    def _():
+        load_run(1, low_ref, kv)
+
+    @pl.when(jnp.logical_and(head == 0, odd_ref[0] == 0))
+    def _():
+        load_run(1, high_ref, kv)
 
     left = lax.broadcasted_iota(jnp.int32, (HD, 2 * BLK), 1) < BLK
     if (1 + slash_ref.shape[1]) % 2:
@@ -274,23 +272,18 @@
                 preferred_element_type=jnp.float32,
             )
             scores = scores * scale + bias_ref[0, pl.ds(block, 1), :split]
-            scores = jnp.concatenate([scores[:, : 2 * BLK] + causal, scores[:, 2 * BLK :]], 1)
             vert_scores = shared[part * BLK : (part + 1) * BLK] * scale
             vert_scores = vert_scores + bias_ref[0, pl.ds(block, 1), split:]
-            row_max = jnp.maximum(
-                jnp.max(scores, axis=1, keepdims=True),
-                jnp.max(vert_scores, axis=1, keepdims=True),
+            scores = jnp.concatenate(
+                [scores[:, : 2 * BLK] + causal, scores[:, 2 * BLK :], vert_scores], 1
             )
-            weights = jnp.exp2(scores - row_max)
-            vert_weights = jnp.exp2(vert_scores - row_max)
-            totals.append(
-                jnp.sum(weights, axis=1, keepdims=True)
-                + jnp.sum(vert_weights, axis=1, keepdims=True)
-            )
-            shared_weights.append(vert_weights.astype(jnp.bfloat16))
+            weights = jnp.exp2(scores - jnp.max(scores, axis=1, keepdims=True))
+            totals.append(jnp.sum(weights, axis=1, keepdims=True))
+            weights = weights.astype(jnp.bfloat16)
+            shared_weights.append(weights[:, split:])
             sums.append(
                 jnp.dot(
-                    weights.astype(jnp.bfloat16),
+                    weights[:, :split],
                     jnp.concatenate(values, 0),
                     preferred_element_type=jnp.float32,
                 )
@@ -309,25 +302,27 @@
     lax.fori_loop(0, blocks // together, one_group, 0, unroll=2)
 
 
-def attend(queries, two_back, low, high, own, odd, vertical, slash, bias, group, kv_heads):
+def attend(queries, two_back, low, high, own, odd, vertical, slash, bias, kv, kv_heads):
     rows = queries.shape[0]
-    q_heads, blocks, width = bias.shape
-    vert_rows = vertical.shape[0] // q_heads
+    _, blocks, width = bias.shape
+    q_heads = slash.shape[0]
+    vert_rows = vertical.shape[0] // (q_heads * kv_heads)
+    base = kv * q_heads
     whole = pl.BlockSpec(own.shape, lambda h, s, o: (0, 0))
     return pl.pallas_call(
-        functools.partial(attend_kernel, group, kv_heads),
+        functools.partial(attend_kernel, kv, kv_heads),
         out_shape=jax.ShapeDtypeStruct((rows, q_heads * HD), queries.dtype),
         grid_spec=pltpu.PrefetchScalarGridSpec(
             num_scalar_prefetch=2,
             grid=(q_heads,),
             in_specs=[
-                pl.BlockSpec((rows, HD), lambda h, s, o: (0, h)),
+                pl.BlockSpec((rows, HD), lambda h, s, o: (0, base + h)),
                 whole,
                 whole,
                 whole,
                 whole,
-                pl.BlockSpec((vert_rows, 2 * HD), lambda h, s, o: (h, 0)),
-                pl.BlockSpec((1, blocks, width), lambda h, s, o: (h, 0, 0)),
+                pl.BlockSpec((vert_rows, 2 * HD), lambda h, s, o: (base + h, 0)),
+                pl.BlockSpec((1, blocks, width), lambda h, s, o: (base + h, 0, 0)),
             ],
             out_specs=pl.BlockSpec((rows, HD), lambda h, s, o: (0, h)),
             scratch_shapes=[
@@ -345,6 +340,31 @@
         ),
         name="attend",
     )(slash, odd, queries, two_back, low, high, own, vertical, bias)
+
+
+def lay_kernel(*refs):
+    out_ref = refs[-1]
+    width = refs[0].shape[1]
+    for place, part_ref in enumerate(refs[:-1]):
+        out_ref[:, place * width : (place + 1) * width] = part_ref[...]
+
+
+def lay_columns(parts, head_count):
+    rows, width = parts[0].shape
+    rows = rows // head_count
+    return pl.pallas_call(
+        lay_kernel,
+        out_shape=jax.ShapeDtypeStruct(
+            (rows, head_count * len(parts) * width), parts[0].dtype
+        ),
+        grid=(head_count,),
+        in_specs=[pl.BlockSpec((rows, width), lambda peer: (peer, 0)) for _ in parts],
+        out_specs=pl.BlockSpec((rows, len(parts) * width), lambda peer: (0, peer)),
+        compiler_params=pltpu.CompilerParams(
+            dimension_semantics=("arbitrary",), vmem_limit_bytes=VMEM_LIMIT // 2
+        ),
+        name="lay_columns",
+    )(*parts)
 
 
 def per_device(queries, key_states, value_states, vertical_blocks, slash_offsets):
@@ -391,22 +411,27 @@
     downward = [(run + 1, run) for run in range(0, run_count - 1, 2)]
     two_back = from_behind(kv_local, "qblk", 2)
     low = lax.ppermute(kv_local, "qblk", upward)
+    two_back, vertical, bias = lax.optimization_barrier((two_back, vertical, bias))
     high = lax.ppermute(two_back, "qblk", downward)
     q_local = lax.all_to_all(queries, "head", split_axis=1, concat_axis=0, tiled=True)
-    attended = attend(
-        q_local,
-        two_back,
-        low,
-        high,
-        kv_local,
-        odd,
-        vertical,
-        slash_mine,
-        bias,
-        group,
-        kv_heads,
-    )
-    return lax.all_to_all(attended, "head", split_axis=0, concat_axis=1, tiled=True)
+    parts = []
+    for kv in range(kv_heads):
+        heads = slice(kv * group, (kv + 1) * group)
+        attended = attend(
+            q_local,
+            two_back,
+            low,
+            high,
+            kv_local,
+            odd,
+            vertical,
+            slash_mine[heads],
+            bias,
+            kv,
+            kv_heads,
+        )
+        parts.append(lax.all_to_all(attended, "head", split_axis=0, concat_axis=0, tiled=True))
+    return lay_columns(parts, head_count)
 
 
 def solution(mesh):

time: 266 us -> 254 us (0.955)
  Pallas kernels: 122 us -> 159 us
  waiting for transfers between devices: 36.4 us -> 5.07 us
  blocking collectives: 81.6 us -> 58.7 us
  starting transfers between devices: 10.2 us -> 13.8 us
    ppermute x1, waiting for transfers between devices: 36.4 us -> 0.01 us  [from_behind(): lax.ppermute(value, axis, [(source, source + steps) for source in range(l...]
    pallas_call x1, Pallas kernels: 30.5 us -> 59.5 us  [sum_up_to_here(): pl.pallas_call(functools.partial(chain_kernel, pieces), out_shape=jax.Sha...]
    all_to_all x1, blocking collectives: 52.4 us -> 29.5 us  [per_device(): lax.all_to_all(attended, 'head', split_axis=0, concat_axis=0, tiled=True)]
    pallas_call x1 -> x3, Pallas kernels: 90.5 us -> 98.2 us  [the longest x2 95.7 us: attend(): pl.pallas_call(functools.partial(attend_kernel, kv, kv_heads), out_shape=...]
    ppermute x1, waiting for transfers between devices: 0.01 us -> 5.06 us  [per_device(): high = lax.ppermute(two_back, 'qblk', downward)]
    unnamed x11 -> x17, local copies, waits for them, and re-layouts: 1.26 us -> 5.08 us
    all_to_all x0 -> x1, starting transfers between devices: none -> 3.61 us  [per_device(): lax.all_to_all(attended, 'head', split_axis=0, concat_axis=0, tiled=True)]
  transfers between devices with their start and end apart: 4 -> 5, of which waited for: 1 -> 1; matrix products, arithmetic and copies ran while one was open for 4% -> 4% of each run, Pallas kernels for 12% -> 43%
where the time goes in v5:
time: 254 us; the launch traced here: 253 us
  Pallas kernels  159 us (63%)
  blocking collectives  58.7 us (23%)
  local copies, waits for them, and re-layouts  15.2 us (6%)
  starting transfers between devices  13.8 us (5%)
  waiting for transfers between devices  5.07 us (2%)
    pallas_call x2, Pallas kernels, attend(): pl.pallas_call(functools.partial(attend_kernel, kv, kv_heads), out_shape=...  95.7 us
    pallas_call x1, Pallas kernels, sum_up_to_here(): pl.pallas_call(functools.partial(chain_kernel, pieces), out_shape=jax.Sha...  59.5 us
    all_to_all x1, blocking collectives, per_device(): lax.all_to_all(attended, 'head', split_axis=0, concat_axis=0, tiled=True)  29.5 us
    all_to_all x1, blocking collectives, per_device(): lax.all_to_all(kv_pair, 'head', split_axis=1, concat_axis=0, tiled=True)  29.2 us
  transfers between devices with their start and end apart: 5, of which 1 were waited for; matrix products, arithmetic and copies ran while one was open for 4% of the time, Pallas kernels for 43%

profile of v5, /device:TPU:24, one launch (start us, length us, event | category | flops | bytes accessed | tf_op | source)
XLA Modules:
  0.0 253.0 jit_solution(6016585167677104949)
XLA Ops:
  0.0 0.0 copy-start
  0.0 1.7 copy_bitcast_fusion.1
  1.7 0.2 pad_maximum_fusion
  1.9 0.0 copy-start.6
  1.9 29.2 %all_to_all.57 = bf16[512,4,512]{2,0,1:T(8,128)(2,1)S(1)} all-to-all(bf16[512,4,512]{2,0,1:T(8,128)(2,1)S(1)} %pad_maximum_fusion), channel_id=1, replica_groups=mesh['head'=4,'qblk'=8] {'head'}, dimensions={1} | all-to-all | bytes 4194304 | tf_op jit(solution)/shard_map/all_to_all | solution.py:389
  31.0 0.0 copy-start.1
  31.0 1.3 collective-permute-start
  32.3 0.0 copy-done.6
  32.3 2.5 copy.42
  34.8 0.0 copy-start.7
  34.8 5.0 %all-to-all-start = ((bf16[512,4,1024]{2,0,1:T(8,128)(2,1)}), bf16[512,4,1024]{2,0,1:T(8,128)(2,1)}, u32[]{:S(2)}, u32[]{:S(2)}) async-start(bf16[512,4,1024]{2,0,1:T(8,128)(2,1)} %bitcast.31), calls=%async_computation | async-start | bytes 8388608 | tf_op jit(solution)/shard_map/all_to_all | solution.py:416
  39.8 0.0 copy-done
  39.8 0.1 constant_dynamic-slice_fusion.1
  39.9 0.0 copy-done.7
  39.9 0.1 broadcast_subtract_fusion.1
  40.0 0.1 copy.35
  40.0 0.1 copy.30
  40.1 0.1 reshape.46.offset_ref
  40.2 0.1 subtract_compare_fusion
  40.3 2.6 %collective-permute-start.1 = (bf16[2048,512]{1,0:T(8,128)(2,1)S(1)}, bf16[2048,512]{1,0:T(8,128)(2,1)}, u32[]{:S(2)}, u32[]{:S(2)}) collective-permute-start(bf16[2048,512]{1,0:T(8,128)(2,1)S(1)} %bitcast.23), channel_id=1, source_target_pairs={{0,1},{2,3},{4,5},{6,7},{8,9},{10,11},{12,13},{14,15},{16,17},{18,... | collective-permute-start | bytes 6291464 | tf_op jit(solution)/shard_map/ppermute | solution.py:413
  42.9 0.0 copy-done.1
  42.9 0.9 pick_vertical.1.own_ref
  43.9 59.5 %sum_up_to_here.1.vert_ref = bf16[2560,256]{1,0:T(8,128)(2,1)S(1)} custom-call(bf16[2560,256]{1,0:T(8,128)(2,1)S(1)} %pick_vertical.1.own_ref), custom_call_target="tpu_custom_call" | custom-call | bytes 41943040 | tf_op jit(solution)/shard_map/sum_up_to_here/pallas_call | solution.py:162
  103.4 0.1 copy.32
  103.5 0.1 broadcast_subtract_fusion
  103.6 0.1 compare_reduce_fusion
  103.7 0.1 not_and_fusion
  103.8 0.7 add_select_fusion
  104.5 0.9 copy.34
  105.5 1.9 broadcast_in_dim.26
  107.4 2.8 %reshape.47.bias_ref = f32[8,32,896]{2,1,0:T(8,128)} reshape(f32[8,32,14,64]{3,2,1,0:T(8,128)} %broadcast_in_dim.26) | data formatting | bytes 1835008 | tf_op jit(solution)/shard_map/reshape | solution.py:408
  110.2 0.0 collective-permute-done.two_ref
  110.2 1.3 collective-permute-start.2
  111.5 0.0 all-to-all-done
  111.5 0.0 collective-permute-done.1.low_ref
  111.5 5.1 %collective-permute-done.2.high_ref = bf16[2048,512]{1,0:T(8,128)(2,1)} collective-permute-done((bf16[2048,512]{1,0:T(8,128)(2,1)}, bf16[2048,512]{1,0:T(8,128)(2,1)}, u32[]{:S(2)}, u32[]{:S(2)}) %collective-permute-start.2) | collective-permute-done | bytes 2097184 | tf_op jit(solution)/shard_map/ppermute | solution.py:415
  116.6 0.0 copy-start.4
  116.6 1.2 copy-done.4
  117.8 47.9 %attend.2 = bf16[2048,512]{1,0:T(8,128)(2,1)S(1)} custom-call(s32[4,8]{1,0:T(4,128)S(1)} %get-tuple-element.18.slash_ref, s32[1]{0:T(128)} %bitcast.odd_ref, bf16[2048,1024]{1,0:T(8,128)(2,1)} %bitcast.2.q_ref, bf16[2048,512]{1,0:T(8,128)(2,1)} %collective-permute-done.two_ref, bf16[2048,512]{1,0:T(8,128)(2,1)} %collective-permute-done.1.low_ref, ...), custom_call_target="tpu_custom_call" | custom-call | flops 3758096384 | bytes 58720256 | tf_op jit(solution)/shard_map/attend/pallas_call | solution.py:312
  165.6 0.0 copy-start.2
  165.7 1.3 copy-done.2
  167.0 3.6 %all-to-all-start.2 = ((bf16[4,512,512]{2,1,0:T(8,128)(2,1)}), bf16[4,512,512]{2,1,0:T(8,128)(2,1)S(1)}, u32[]{:S(2)}, u32[]{:S(2)}) async-start(bf16[4,512,512]{2,1,0:T(8,128)(2,1)} %bitcast.29), calls=%async_computation.2 | async-start | bytes 4194304 | tf_op jit(solution)/shard_map/all_to_all | solution.py:433
  170.6 0.0 copy-start.5
  170.6 1.2 copy-done.5
  171.8 47.9 %attend.3 = bf16[2048,512]{1,0:T(8,128)(2,1)S(1)} custom-call(s32[4,8]{1,0:T(4,128)S(1)} %get-tuple-element.17.slash_ref, s32[1]{0:T(128)} %bitcast.odd_ref, bf16[2048,1024]{1,0:T(8,128)(2,1)} %bitcast.2.q_ref, bf16[2048,512]{1,0:T(8,128)(2,1)} %collective-permute-done.two_ref, bf16[2048,512]{1,0:T(8,128)(2,1)} %collective-permute-done.1.low_ref, ...), custom_call_target="tpu_custom_call" | custom-call | flops 3758096384 | bytes 58720256 | tf_op jit(solution)/shard_map/attend/pallas_call | solution.py:312
  219.7 0.0 copy-start.3
  219.7 1.3 copy-done.3
  221.0 0.0 all-to-all-done.2
  221.0 29.5 %all_to_all.58 = bf16[4,512,512]{2,1,0:T(8,128)(2,1)S(1)} all-to-all(bf16[4,512,512]{2,1,0:T(8,128)(2,1)} %bitcast.30), channel_id=1, replica_groups=mesh['head'=4,'qblk'=8] {'head'}, dimensions={0} | all-to-all | bytes 4194304 | tf_op jit(solution)/shard_map/all_to_all | solution.py:433
  250.5 2.4 lay_columns.1
  (4 shorter events, 0.0 us)
Async XLA Ops:
  0.0 39.8 %copy-start = (s32[32,8]{0,1:T(8,128)S(1)}, s32[32,8]{0,1:T(8,128)}, u32[]{:S(2)}) copy-start(s32[32,8]{0,1:T(8,128)} %param.9) | copy-start | bytes 3076
  1.9 30.5 %copy-start.6 = (bf16[512,4096]{1,0:T(8,128)(2,1)S(1)}, bf16[512,4096]{1,0:T(8,128)(2,1)}, u32[]{:S(2)}) copy-start(bf16[512,4096]{1,0:T(8,128)(2,1)} %param.5) | copy-start | bytes 12582916
  31.0 11.9 %copy-start.1 = (bf16[512,4,512]{2,0,1:T(8,128)(2,1)}, bf16[512,4,512]{2,0,1:T(8,128)(2,1)S(1)}, u32[]{:S(2)}) copy-start(bf16[512,4,512]{2,0,1:T(8,128)(2,1)S(1)} %all_to_all.57) | copy-start | bytes 6291460
  31.0 79.2 %collective-permute-start = (bf16[2048,512]{1,0:T(8,128)(2,1)S(1)}, bf16[2048,512]{1,0:T(8,128)(2,1)}, u32[]{:S(2)}, u32[]{:S(2)}) collective-permute-start(bf16[2048,512]{1,0:T(8,128)(2,1)S(1)} %bitcast.22), channel_id=1, source_target_pairs={{0,2},{1,3},{2,4},{3,5},{4,6},{5,7},{8,10},{9,11},{10,12},{11,13},... | collective-permute-start | bytes 6291464 | tf_op jit(solution)/shard_map/ppermute | solution.py:22
  34.8 5.1 %copy-start.7 = (s32[32,5]{0,1:T(8,128)S(1)}, s32[32,5]{0,1:T(8,128)}, u32[]{:S(2)}) copy-start(s32[32,5]{0,1:T(8,128)} %param.8) | copy-start | bytes 1924
  34.8 76.7 %all-to-all-start = ((bf16[512,4,1024]{2,0,1:T(8,128)(2,1)}), bf16[512,4,1024]{2,0,1:T(8,128)(2,1)}, u32[]{:S(2)}, u32[]{:S(2)}) async-start(bf16[512,4,1024]{2,0,1:T(8,128)(2,1)} %bitcast.31), calls=%async_computation | async-start | bytes 8388608 | tf_op jit(solution)/shard_map/all_to_all | solution.py:416
  40.3 71.2 %collective-permute-start.1 = (bf16[2048,512]{1,0:T(8,128)(2,1)S(1)}, bf16[2048,512]{1,0:T(8,128)(2,1)}, u32[]{:S(2)}, u32[]{:S(2)}) collective-permute-start(bf16[2048,512]{1,0:T(8,128)(2,1)S(1)} %bitcast.23), channel_id=1, source_target_pairs={{0,1},{2,3},{4,5},{6,7},{8,9},{10,11},{12,13},{14,15},{16,17},{18,... | collective-permute-start | bytes 6291464 | tf_op jit(solution)/shard_map/ppermute | solution.py:413
  110.2 6.4 %collective-permute-start.2 = (bf16[2048,512]{1,0:T(8,128)(2,1)}, bf16[2048,512]{1,0:T(8,128)(2,1)}, u32[]{:S(2)}, u32[]{:S(2)}) collective-permute-start(bf16[2048,512]{1,0:T(8,128)(2,1)} %collective-permute-done.two_ref), channel_id=1, source_target_pairs={{1,0},{3,2},{5,4},{7,6},{9,8},{11,10},{13,12},{15,14},{17,16},{19,... | collective-permute-start | bytes 6291464 | tf_op jit(solution)/shard_map/ppermute | solution.py:415
  116.6 1.2 copy-start.4
  165.6 1.3 copy-start.2
  167.0 54.0 %all-to-all-start.2 = ((bf16[4,512,512]{2,1,0:T(8,128)(2,1)}), bf16[4,512,512]{2,1,0:T(8,128)(2,1)S(1)}, u32[]{:S(2)}, u32[]{:S(2)}) async-start(bf16[4,512,512]{2,1,0:T(8,128)(2,1)} %bitcast.29), calls=%async_computation.2 | async-start | bytes 4194304 | tf_op jit(solution)/shard_map/all_to_all | solution.py:433
  170.6 1.2 copy-start.5
  219.7 1.3 copy-start.3

commit v6 on v5

--- a/solution.py
+++ b/solution.py
@@ -252,12 +252,12 @@
             (((1,), (1,)), ((), ())),
             preferred_element_type=jnp.float32,
         )
-        sums, totals, shared_weights = [], [], []
-        for part in range(together):
+        parts = range(together)
+        group_scores, group_values = [], []
+        for part in parts:
             block = step * together + part
             row = pl.multiple_of(block * BLK, BLK)
             starts = [pl.multiple_of((front + block - offset) * BLK, BLK) for offset in offsets]
-
             halves = [key_ref[front + block - offset] for offset in offsets] + lead_keys
             keys = [
                 jnp.where(left, halves[pair], halves[pair + 1])
@@ -266,28 +266,38 @@
             values = [value_ref[pl.ds(start, BLK), :] for start in starts]
             if lead:
                 values.append(vert_ref[:lead, HD:])
-            scores = jnp.dot(
-                q_ref[pl.ds(row, BLK), :],
-                jnp.concatenate(keys, 1),
-                preferred_element_type=jnp.float32,
-            )
-            scores = scores * scale + bias_ref[0, pl.ds(block, 1), :split]
-            vert_scores = shared[part * BLK : (part + 1) * BLK] * scale
-            vert_scores = vert_scores + bias_ref[0, pl.ds(block, 1), split:]
-            scores = jnp.concatenate(
-                [scores[:, : 2 * BLK] + causal, scores[:, 2 * BLK :], vert_scores], 1
-            )
-            weights = jnp.exp2(scores - jnp.max(scores, axis=1, keepdims=True))
-            totals.append(jnp.sum(weights, axis=1, keepdims=True))
-            weights = weights.astype(jnp.bfloat16)
-            shared_weights.append(weights[:, split:])
-            sums.append(
+            group_values.append(values)
+            group_scores.append(
                 jnp.dot(
-                    weights[:, :split],
-                    jnp.concatenate(values, 0),
+                    q_ref[pl.ds(row, BLK), :],
+                    jnp.concatenate(keys, 1),
                     preferred_element_type=jnp.float32,
                 )
             )
+        masked, tops, weights = [], [], []
+        for part in parts:
+            block = step * together + part
+            scores = jnp.concatenate(
+                [group_scores[part], shared[part * BLK : (part + 1) * BLK]], 1
+            )
+            scores = scores * scale + bias_ref[0, pl.ds(block, 1), :]
+            masked.append(
+                jnp.concatenate([scores[:, : 2 * BLK] + causal, scores[:, 2 * BLK :]], 1)
+            )
+            tops.append(jnp.max(masked[part], axis=1, keepdims=True))
+        for part in parts:
+            weights.append(jnp.exp2(masked[part] - tops[part]))
+        totals = [jnp.sum(weights[part], axis=1, keepdims=True) for part in parts]
+        weights = [weights[part].astype(jnp.bfloat16) for part in parts]
+        sums = [
+            jnp.dot(
+                weights[part][:, :split],
+                jnp.concatenate(group_values[part], 0),
+                preferred_element_type=jnp.float32,
+            )
+            for part in parts
+        ]
+        shared_weights = [weights[part][:, split:] for part in parts]
         summed = jnp.dot(
             jnp.concatenate(shared_weights, 0),
             vert_ref[lead:, HD:],
@@ -394,7 +404,6 @@
     first_block = block_index * blocks
     own_vertical = pick_vertical(kv_local, vert_mine - first_block, group, kv_heads)
     own_vertical, vert_mine = lax.optimization_barrier((own_vertical, vert_mine))
-    vertical = sum_up_to_here(own_vertical)
     odd = lax.rem(block_index, 2).astype(jnp.int32).reshape(1)
 
     block_ids = first_block + jnp.arange(blocks, dtype=jnp.int32)
@@ -411,7 +420,9 @@
     downward = [(run + 1, run) for run in range(0, run_count - 1, 2)]
     two_back = from_behind(kv_local, "qblk", 2)
     low = lax.ppermute(kv_local, "qblk", upward)
-    two_back, vertical, bias = lax.optimization_barrier((two_back, vertical, bias))
+    own_vertical, bias = lax.optimization_barrier((own_vertical, bias))
+    vertical = sum_up_to_here(own_vertical)
+    two_back, vertical = lax.optimization_barrier((two_back, vertical))
     high = lax.ppermute(two_back, "qblk", downward)
     q_local = lax.all_to_all(queries, "head", split_axis=1, concat_axis=0, tiled=True)
     parts = []

time: 254 us -> 207 us (0.81)
  Pallas kernels: 159 us -> 111 us
    pallas_call x2, Pallas kernels: 95.7 us -> 56.2 us  [attend(): pl.pallas_call(functools.partial(attend_kernel, kv, kv_heads), out_shape=...]
    pallas_call x1, Pallas kernels: 59.5 us -> 51.8 us  [sum_up_to_here(): pl.pallas_call(functools.partial(chain_kernel, pieces), out_shape=jax.Sha...]
    unnamed x17 -> x21, local copies, waits for them, and re-layouts: 5.08 us -> 7.51 us
  transfers between devices with their start and end apart: 5 -> 5, of which waited for: 1 -> 1; matrix products, arithmetic and copies ran while one was open for 4% -> 4% of each run, Pallas kernels for 43% -> 39%
where the time goes in v6:
time: 207 us
  Pallas kernels  111 us (54%)
  blocking collectives  58.7 us (28%)
  local copies, waits for them, and re-layouts  16.8 us (8%)
  starting transfers between devices  13.8 us (7%)
  waiting for transfers between devices  5.07 us (2%)
    pallas_call x2, Pallas kernels, attend(): pl.pallas_call(functools.partial(attend_kernel, kv, kv_heads), out_shape=...  56.2 us
    pallas_call x1, Pallas kernels, sum_up_to_here(): pl.pallas_call(functools.partial(chain_kernel, pieces), out_shape=jax.Sha...  51.8 us
    all_to_all x1, blocking collectives, per_device(): lax.all_to_all(attended, 'head', split_axis=0, concat_axis=0, tiled=True)  29.5 us
    all_to_all x1, blocking collectives, per_device(): lax.all_to_all(kv_pair, 'head', split_axis=1, concat_axis=0, tiled=True)  29.2 us
    unnamed x21, local copies, waits for them, and re-layouts  7.51 us
    ppermute x1, waiting for transfers between devices, per_device(): high = lax.ppermute(two_back, 'qblk', downward)  5.06 us
    all_to_all x1, starting transfers between devices, per_device(): lax.all_to_all(queries, 'head', split_axis=1, concat_axis=0, tiled=True)  4.99 us
  transfers between devices with their start and end apart: 5, of which 1 were waited for; matrix products, arithmetic and copies ran while one was open for 4% of the time, Pallas kernels for 39%

profile of v6, /device:TPU:24, one launch (start us, length us, event | category | flops | bytes accessed | tf_op | source)
XLA Modules:
  0.0 206.7 jit_solution(478734447840709790)
XLA Ops:
  0.0 0.0 copy-start
  0.0 1.7 copy_bitcast_fusion.1
  1.7 0.2 pad_maximum_fusion
  1.9 0.0 copy-start.8
  1.9 29.2 %all_to_all.57 = bf16[512,4,512]{2,0,1:T(8,128)(2,1)S(1)} all-to-all(bf16[512,4,512]{2,0,1:T(8,128)(2,1)S(1)} %pad_maximum_fusion), channel_id=1, replica_groups=mesh['head'=4,'qblk'=8] {'head'}, dimensions={1} | all-to-all | bytes 4194304 | tf_op jit(solution)/shard_map/all_to_all | solution.py:399
  31.0 0.0 copy-start.1
  31.0 1.3 collective-permute-start
  32.3 0.0 copy-done.8
  32.3 2.5 %copy.42 = bf16[64,4,8,1024]{3,2,0,1:T(8,128)(2,1)} copy(bf16[64,4,8,1024]{3,2,1,0:T(8,128)(2,1)S(1)} %bitcast.32) | data formatting | bytes 8388608 | tf_op jit(solution)/shard_map/all_to_all | solution.py:427
  34.8 0.0 copy-start.9
  34.8 5.0 %all-to-all-start = ((bf16[512,4,1024]{2,0,1:T(8,128)(2,1)}), bf16[512,4,1024]{2,0,1:T(8,128)(2,1)}, u32[]{:S(2)}, u32[]{:S(2)}) async-start(bf16[512,4,1024]{2,0,1:T(8,128)(2,1)} %bitcast.31), calls=%async_computation | async-start | bytes 8388608 | tf_op jit(solution)/shard_map/all_to_all | solution.py:427
  39.8 0.0 copy-done
  39.8 0.1 constant_dynamic-slice_fusion.1
  39.9 0.0 copy-done.9
  39.9 0.1 broadcast_subtract_fusion.1
  40.0 0.1 copy.35
  40.0 0.1 copy.30
  40.1 0.1 reshape.46.offset_ref
  40.2 0.1 subtract_compare_fusion
  40.3 2.6 %collective-permute-start.1 = (bf16[2048,512]{1,0:T(8,128)(2,1)S(1)}, bf16[2048,512]{1,0:T(8,128)(2,1)}, u32[]{:S(2)}, u32[]{:S(2)}) collective-permute-start(bf16[2048,512]{1,0:T(8,128)(2,1)S(1)} %bitcast.23), channel_id=1, source_target_pairs={{0,1},{2,3},{4,5},{6,7},{8,9},{10,11},{12,13},{14,15},{16,17},{18,... | collective-permute-start | bytes 6291464 | tf_op jit(solution)/shard_map/ppermute | solution.py:422
  42.9 0.0 copy-done.1
  42.9 0.9 pick_vertical.1.own_ref
  43.9 0.0 copy-start.6
  43.9 1.1 copy-done.6
  45.0 0.1 copy.32
  45.1 0.1 broadcast_subtract_fusion
  45.2 0.1 compare_reduce_fusion
  45.3 0.1 not_and_fusion
  45.4 0.1 add_select_fusion
  45.5 0.1 copy.34
  45.6 1.9 broadcast_in_dim.26
  47.6 2.8 %reshape.47.bias_ref = f32[8,32,896]{2,1,0:T(8,128)} reshape(f32[8,32,14,64]{3,2,1,0:T(8,128)} %broadcast_in_dim.26) | data formatting | bytes 1835008 | tf_op jit(solution)/shard_map/reshape | solution.py:417
  50.3 0.0 copy-start.7
  50.3 1.3 copy-done.7
  51.6 51.8 %sum_up_to_here.1.vert_ref = bf16[2560,256]{1,0:T(8,128)(2,1)S(1)} custom-call(bf16[2560,256]{1,0:T(8,128)(2,1)S(1)} %copy-done.7), custom_call_target="tpu_custom_call" | custom-call | bytes 41943040 | tf_op jit(solution)/shard_map/sum_up_to_here/pallas_call | solution.py:162
  103.4 0.0 collective-permute-done.two_ref
  103.4 1.3 collective-permute-start.2
  104.7 0.0 all-to-all-done
  104.8 0.0 collective-permute-done.1.low_ref
  104.8 5.1 %collective-permute-done.2.high_ref = bf16[2048,512]{1,0:T(8,128)(2,1)} collective-permute-done((bf16[2048,512]{1,0:T(8,128)(2,1)}, bf16[2048,512]{1,0:T(8,128)(2,1)}, u32[]{:S(2)}, u32[]{:S(2)}) %collective-permute-start.2) | collective-permute-done | bytes 2097184 | tf_op jit(solution)/shard_map/ppermute | solution.py:426
  109.8 0.0 copy-start.4
  109.8 1.2 copy-done.4
  111.0 28.1 %attend.2 = bf16[2048,512]{1,0:T(8,128)(2,1)S(1)} custom-call(s32[4,8]{1,0:T(4,128)S(1)} %get-tuple-element.20.slash_ref, s32[1]{0:T(128)} %bitcast.odd_ref, bf16[2048,1024]{1,0:T(8,128)(2,1)} %bitcast.2.q_ref, bf16[2048,512]{1,0:T(8,128)(2,1)} %collective-permute-done.two_ref, bf16[2048,512]{1,0:T(8,128)(2,1)} %collective-permute-done.1.low_ref, ...), custom_call_target="tpu_custom_call" | custom-call | flops 3758096384 | bytes 58720256 | tf_op jit(solution)/shard_map/attend/pallas_call | solution.py:322
  139.1 0.0 copy-start.2
  139.1 1.3 copy-done.2
  140.4 3.6 %all-to-all-start.2 = ((bf16[4,512,512]{2,1,0:T(8,128)(2,1)}), bf16[4,512,512]{2,1,0:T(8,128)(2,1)S(1)}, u32[]{:S(2)}, u32[]{:S(2)}) async-start(bf16[4,512,512]{2,1,0:T(8,128)(2,1)} %bitcast.29), calls=%async_computation.2 | async-start | bytes 4194304 | tf_op jit(solution)/shard_map/all_to_all | solution.py:444
  144.1 0.0 copy-start.5
  144.1 1.2 copy-done.5
  145.2 28.1 %attend.3 = bf16[2048,512]{1,0:T(8,128)(2,1)S(1)} custom-call(s32[4,8]{1,0:T(4,128)S(1)} %get-tuple-element.19.slash_ref, s32[1]{0:T(128)} %bitcast.odd_ref, bf16[2048,1024]{1,0:T(8,128)(2,1)} %bitcast.2.q_ref, bf16[2048,512]{1,0:T(8,128)(2,1)} %collective-permute-done.two_ref, bf16[2048,512]{1,0:T(8,128)(2,1)} %collective-permute-done.1.low_ref, ...), custom_call_target="tpu_custom_call" | custom-call | flops 3758096384 | bytes 58720256 | tf_op jit(solution)/shard_map/attend/pallas_call | solution.py:322
  173.3 0.0 copy-start.3
  173.3 1.3 copy-done.3
  174.7 0.0 all-to-all-done.2
  174.7 29.5 %all_to_all.58 = bf16[4,512,512]{2,1,0:T(8,128)(2,1)S(1)} all-to-all(bf16[4,512,512]{2,1,0:T(8,128)(2,1)} %bitcast.30), channel_id=1, replica_groups=mesh['head'=4,'qblk'=8] {'head'}, dimensions={0} | all-to-all | bytes 4194304 | tf_op jit(solution)/shard_map/all_to_all | solution.py:444
  204.2 2.4 %lay_columns.1 = bf16[512,4096]{1,0:T(8,128)(2,1)} custom-call(bf16[2048,512]{1,0:T(8,128)(2,1)S(1)} %bitcast.27, bf16[2048,512]{1,0:T(8,128)(2,1)S(1)} %bitcast.28), custom_call_target="tpu_custom_call" | custom-call | tf_op jit(solution)/shard_map/lay_columns/pallas_call | solution.py:365
  (4 shorter events, 0.0 us)
Async XLA Ops:
  0.0 39.8 %copy-start = (s32[32,8]{0,1:T(8,128)S(1)}, s32[32,8]{0,1:T(8,128)}, u32[]{:S(2)}) copy-start(s32[32,8]{0,1:T(8,128)} %param.9) | copy-start | bytes 3076
  1.9 30.5 %copy-start.8 = (bf16[512,4096]{1,0:T(8,128)(2,1)S(1)}, bf16[512,4096]{1,0:T(8,128)(2,1)}, u32[]{:S(2)}) copy-start(bf16[512,4096]{1,0:T(8,128)(2,1)} %param.5) | copy-start | bytes 12582916
  31.0 11.9 %copy-start.1 = (bf16[512,4,512]{2,0,1:T(8,128)(2,1)}, bf16[512,4,512]{2,0,1:T(8,128)(2,1)S(1)}, u32[]{:S(2)}) copy-start(bf16[512,4,512]{2,0,1:T(8,128)(2,1)S(1)} %all_to_all.57) | copy-start | bytes 6291460
  31.0 72.4 %collective-permute-start = (bf16[2048,512]{1,0:T(8,128)(2,1)S(1)}, bf16[2048,512]{1,0:T(8,128)(2,1)}, u32[]{:S(2)}, u32[]{:S(2)}) collective-permute-start(bf16[2048,512]{1,0:T(8,128)(2,1)S(1)} %bitcast.22), channel_id=1, source_target_pairs={{0,2},{1,3},{2,4},{3,5},{4,6},{5,7},{8,10},{9,11},{10,12},{11,13},... | collective-permute-start | bytes 6291464 | tf_op jit(solution)/shard_map/ppermute | solution.py:22
  34.8 5.1 %copy-start.9 = (s32[32,5]{0,1:T(8,128)S(1)}, s32[32,5]{0,1:T(8,128)}, u32[]{:S(2)}) copy-start(s32[32,5]{0,1:T(8,128)} %param.8) | copy-start | bytes 1924
  34.8 69.9 %all-to-all-start = ((bf16[512,4,1024]{2,0,1:T(8,128)(2,1)}), bf16[512,4,1024]{2,0,1:T(8,128)(2,1)}, u32[]{:S(2)}, u32[]{:S(2)}) async-start(bf16[512,4,1024]{2,0,1:T(8,128)(2,1)} %bitcast.31), calls=%async_computation | async-start | bytes 8388608 | tf_op jit(solution)/shard_map/all_to_all | solution.py:427
  40.3 64.5 %collective-permute-start.1 = (bf16[2048,512]{1,0:T(8,128)(2,1)S(1)}, bf16[2048,512]{1,0:T(8,128)(2,1)}, u32[]{:S(2)}, u32[]{:S(2)}) collective-permute-start(bf16[2048,512]{1,0:T(8,128)(2,1)S(1)} %bitcast.23), channel_id=1, source_target_pairs={{0,1},{2,3},{4,5},{6,7},{8,9},{10,11},{12,13},{14,15},{16,17},{18,... | collective-permute-start | bytes 6291464 | tf_op jit(solution)/shard_map/ppermute | solution.py:422
  43.9 1.1 copy-start.6
  50.3 1.3 copy-start.7
  103.4 6.4 %collective-permute-start.2 = (bf16[2048,512]{1,0:T(8,128)(2,1)}, bf16[2048,512]{1,0:T(8,128)(2,1)}, u32[]{:S(2)}, u32[]{:S(2)}) collective-permute-start(bf16[2048,512]{1,0:T(8,128)(2,1)} %collective-permute-done.two_ref), channel_id=1, source_target_pairs={{1,0},{3,2},{5,4},{7,6},{9,8},{11,10},{13,12},{15,14},{17,16},{19,... | collective-permute-start | bytes 6291464 | tf_op jit(solution)/shard_map/ppermute | solution.py:426
  109.8 1.2 copy-start.4
  139.1 1.3 copy-start.2
  140.4 34.2 %all-to-all-start.2 = ((bf16[4,512,512]{2,1,0:T(8,128)(2,1)}), bf16[4,512,512]{2,1,0:T(8,128)(2,1)S(1)}, u32[]{:S(2)}, u32[]{:S(2)}) async-start(bf16[4,512,512]{2,1,0:T(8,128)(2,1)} %bitcast.29), calls=%async_computation.2 | async-start | bytes 4194304 | tf_op jit(solution)/shard_map/all_to_all | solution.py:444
  144.1 1.2 copy-start.5
  173.3 1.3 copy-start.3

commit v7 on v6

--- a/solution.py
+++ b/solution.py
@@ -242,7 +242,7 @@
     offsets = [0] + [slash_ref[head, slot] for slot in range(slash_count)]
     lead = (1 + slash_count) % 2 * BLK
     split = (1 + slash_count) * BLK + lead
-    together = 4 if blocks % 4 == 0 else 1
+    together = next(count for count in (8, 4, 2, 1) if blocks % count == 0)
 
     def one_group(step, carry):
         base = pl.multiple_of(step * together * BLK, BLK)
@@ -309,7 +309,7 @@
         ).astype(out_ref.dtype)
         return carry
 
-    lax.fori_loop(0, blocks // together, one_group, 0, unroll=2)
+    lax.fori_loop(0, blocks // together, one_group, 0)
 
 
 def attend(queries, two_back, low, high, own, odd, vertical, slash, bias, kv, kv_heads):

time: 207 us -> 207 us (level)
  no operation moved by 1% of the time
where the time goes in v7:
time: 207 us; the launch traced here: 206 us
  Pallas kernels  111 us (54%)
  blocking collectives  58.7 us (28%)
  local copies, waits for them, and re-layouts  16.8 us (8%)
  starting transfers between devices  13.8 us (7%)
  waiting for transfers between devices  5.07 us (2%)
    pallas_call x2, Pallas kernels, attend(): pl.pallas_call(functools.partial(attend_kernel, kv, kv_heads), out_shape=...  55.7 us
    pallas_call x1, Pallas kernels, sum_up_to_here(): pl.pallas_call(functools.partial(chain_kernel, pieces), out_shape=jax.Sha...  51.8 us
    all_to_all x1, blocking collectives, per_device(): lax.all_to_all(attended, 'head', split_axis=0, concat_axis=0, tiled=True)  29.6 us
    all_to_all x1, blocking collectives, per_device(): lax.all_to_all(kv_pair, 'head', split_axis=1, concat_axis=0, tiled=True)  29.2 us
    unnamed x21, local copies, waits for them, and re-layouts  7.51 us
    ppermute x1, waiting for transfers between devices, per_device(): high = lax.ppermute(two_back, 'qblk', downward)  5.06 us
    all_to_all x1, starting transfers between devices, per_device(): lax.all_to_all(queries, 'head', split_axis=1, concat_axis=0, tiled=True)  4.99 us
  transfers between devices with their start and end apart: 5, of which 1 were waited for; matrix products, arithmetic and copies ran while one was open for 4% of the time, Pallas kernels for 39%

profile of v7, /device:TPU:24, one launch (start us, length us, event | category | flops | bytes accessed | tf_op | source)
XLA Modules:
  0.0 206.3 jit_solution(1766604874840923477)
XLA Ops:
  0.0 0.0 copy-start
  0.0 1.7 copy_bitcast_fusion.1
  1.7 0.2 pad_maximum_fusion
  1.9 0.0 copy-start.8
  1.9 29.2 %all_to_all.57 = bf16[512,4,512]{2,0,1:T(8,128)(2,1)S(1)} all-to-all(bf16[512,4,512]{2,0,1:T(8,128)(2,1)S(1)} %pad_maximum_fusion), channel_id=1, replica_groups=mesh['head'=4,'qblk'=8] {'head'}, dimensions={1} | all-to-all | bytes 4194304 | tf_op jit(solution)/shard_map/all_to_all | solution.py:399
  31.0 0.0 copy-start.1
  31.0 1.3 collective-permute-start
  32.3 0.0 copy-done.8
  32.3 2.5 %copy.42 = bf16[64,4,8,1024]{3,2,0,1:T(8,128)(2,1)} copy(bf16[64,4,8,1024]{3,2,1,0:T(8,128)(2,1)S(1)} %bitcast.32) | data formatting | bytes 8388608 | tf_op jit(solution)/shard_map/all_to_all | solution.py:427
  34.8 0.0 copy-start.9
  34.8 5.0 %all-to-all-start = ((bf16[512,4,1024]{2,0,1:T(8,128)(2,1)}), bf16[512,4,1024]{2,0,1:T(8,128)(2,1)}, u32[]{:S(2)}, u32[]{:S(2)}) async-start(bf16[512,4,1024]{2,0,1:T(8,128)(2,1)} %bitcast.31), calls=%async_computation | async-start | bytes 8388608 | tf_op jit(solution)/shard_map/all_to_all | solution.py:427
  39.8 0.0 copy-done
  39.8 0.1 constant_dynamic-slice_fusion.1
  39.9 0.0 copy-done.9
  39.9 0.1 broadcast_subtract_fusion.1
  40.0 0.1 copy.35
  40.0 0.1 copy.30
  40.1 0.1 reshape.46.offset_ref
  40.2 0.1 subtract_compare_fusion
  40.3 2.6 %collective-permute-start.1 = (bf16[2048,512]{1,0:T(8,128)(2,1)S(1)}, bf16[2048,512]{1,0:T(8,128)(2,1)}, u32[]{:S(2)}, u32[]{:S(2)}) collective-permute-start(bf16[2048,512]{1,0:T(8,128)(2,1)S(1)} %bitcast.23), channel_id=1, source_target_pairs={{0,1},{2,3},{4,5},{6,7},{8,9},{10,11},{12,13},{14,15},{16,17},{18,... | collective-permute-start | bytes 6291464 | tf_op jit(solution)/shard_map/ppermute | solution.py:422
  42.9 0.0 copy-done.1
  42.9 0.9 pick_vertical.1.own_ref
  43.9 0.0 copy-start.6
  43.9 1.1 copy-done.6
  45.0 0.1 copy.32
  45.1 0.1 broadcast_subtract_fusion
  45.2 0.1 compare_reduce_fusion
  45.3 0.1 not_and_fusion
  45.4 0.1 add_select_fusion
  45.5 0.1 copy.34
  45.6 1.9 broadcast_in_dim.26
  47.6 2.8 %reshape.47.bias_ref = f32[8,32,896]{2,1,0:T(8,128)} reshape(f32[8,32,14,64]{3,2,1,0:T(8,128)} %broadcast_in_dim.26) | data formatting | bytes 1835008 | tf_op jit(solution)/shard_map/reshape | solution.py:417
  50.3 0.0 copy-start.7
  50.3 1.3 copy-done.7
  51.6 51.8 %sum_up_to_here.1.vert_ref = bf16[2560,256]{1,0:T(8,128)(2,1)S(1)} custom-call(bf16[2560,256]{1,0:T(8,128)(2,1)S(1)} %copy-done.7), custom_call_target="tpu_custom_call" | custom-call | bytes 41943040 | tf_op jit(solution)/shard_map/sum_up_to_here/pallas_call | solution.py:162
  103.4 0.0 collective-permute-done.two_ref
  103.4 1.3 collective-permute-start.2
  104.7 0.0 all-to-all-done
  104.8 0.0 collective-permute-done.1.low_ref
  104.8 5.1 %collective-permute-done.2.high_ref = bf16[2048,512]{1,0:T(8,128)(2,1)} collective-permute-done((bf16[2048,512]{1,0:T(8,128)(2,1)}, bf16[2048,512]{1,0:T(8,128)(2,1)}, u32[]{:S(2)}, u32[]{:S(2)}) %collective-permute-start.2) | collective-permute-done | bytes 2097184 | tf_op jit(solution)/shard_map/ppermute | solution.py:426
  109.8 0.0 copy-start.4
  109.8 1.2 copy-done.4
  111.0 27.9 %attend.2 = bf16[2048,512]{1,0:T(8,128)(2,1)S(1)} custom-call(s32[4,8]{1,0:T(4,128)S(1)} %get-tuple-element.20.slash_ref, s32[1]{0:T(128)} %bitcast.odd_ref, bf16[2048,1024]{1,0:T(8,128)(2,1)} %bitcast.2.q_ref, bf16[2048,512]{1,0:T(8,128)(2,1)} %collective-permute-done.two_ref, bf16[2048,512]{1,0:T(8,128)(2,1)} %collective-permute-done.1.low_ref, ...), custom_call_target="tpu_custom_call" | custom-call | flops 3758096384 | bytes 58720256 | tf_op jit(solution)/shard_map/attend/pallas_call | solution.py:322
  138.9 0.0 copy-start.2
  138.9 1.3 copy-done.2
  140.2 3.6 %all-to-all-start.2 = ((bf16[4,512,512]{2,1,0:T(8,128)(2,1)}), bf16[4,512,512]{2,1,0:T(8,128)(2,1)S(1)}, u32[]{:S(2)}, u32[]{:S(2)}) async-start(bf16[4,512,512]{2,1,0:T(8,128)(2,1)} %bitcast.29), calls=%async_computation.2 | async-start | bytes 4194304 | tf_op jit(solution)/shard_map/all_to_all | solution.py:444
  143.8 0.0 copy-start.5
  143.8 1.2 copy-done.5
  145.0 27.9 %attend.3 = bf16[2048,512]{1,0:T(8,128)(2,1)S(1)} custom-call(s32[4,8]{1,0:T(4,128)S(1)} %get-tuple-element.19.slash_ref, s32[1]{0:T(128)} %bitcast.odd_ref, bf16[2048,1024]{1,0:T(8,128)(2,1)} %bitcast.2.q_ref, bf16[2048,512]{1,0:T(8,128)(2,1)} %collective-permute-done.two_ref, bf16[2048,512]{1,0:T(8,128)(2,1)} %collective-permute-done.1.low_ref, ...), custom_call_target="tpu_custom_call" | custom-call | flops 3758096384 | bytes 58720256 | tf_op jit(solution)/shard_map/attend/pallas_call | solution.py:322
  172.9 0.0 copy-start.3
  172.9 1.3 copy-done.3
  174.2 0.0 all-to-all-done.2
  174.2 29.6 %all_to_all.58 = bf16[4,512,512]{2,1,0:T(8,128)(2,1)S(1)} all-to-all(bf16[4,512,512]{2,1,0:T(8,128)(2,1)} %bitcast.30), channel_id=1, replica_groups=mesh['head'=4,'qblk'=8] {'head'}, dimensions={0} | all-to-all | bytes 4194304 | tf_op jit(solution)/shard_map/all_to_all | solution.py:444
  203.8 2.4 %lay_columns.1 = bf16[512,4096]{1,0:T(8,128)(2,1)} custom-call(bf16[2048,512]{1,0:T(8,128)(2,1)S(1)} %bitcast.27, bf16[2048,512]{1,0:T(8,128)(2,1)S(1)} %bitcast.28), custom_call_target="tpu_custom_call" | custom-call | tf_op jit(solution)/shard_map/lay_columns/pallas_call | solution.py:365
  (4 shorter events, 0.0 us)
Async XLA Ops:
  0.0 39.8 %copy-start = (s32[32,8]{0,1:T(8,128)S(1)}, s32[32,8]{0,1:T(8,128)}, u32[]{:S(2)}) copy-start(s32[32,8]{0,1:T(8,128)} %param.9) | copy-start | bytes 3076
  1.9 30.5 %copy-start.8 = (bf16[512,4096]{1,0:T(8,128)(2,1)S(1)}, bf16[512,4096]{1,0:T(8,128)(2,1)}, u32[]{:S(2)}) copy-start(bf16[512,4096]{1,0:T(8,128)(2,1)} %param.5) | copy-start | bytes 12582916
  31.0 11.9 %copy-start.1 = (bf16[512,4,512]{2,0,1:T(8,128)(2,1)}, bf16[512,4,512]{2,0,1:T(8,128)(2,1)S(1)}, u32[]{:S(2)}) copy-start(bf16[512,4,512]{2,0,1:T(8,128)(2,1)S(1)} %all_to_all.57) | copy-start | bytes 6291460
  31.0 72.4 %collective-permute-start = (bf16[2048,512]{1,0:T(8,128)(2,1)S(1)}, bf16[2048,512]{1,0:T(8,128)(2,1)}, u32[]{:S(2)}, u32[]{:S(2)}) collective-permute-start(bf16[2048,512]{1,0:T(8,128)(2,1)S(1)} %bitcast.22), channel_id=1, source_target_pairs={{0,2},{1,3},{2,4},{3,5},{4,6},{5,7},{8,10},{9,11},{10,12},{11,13},... | collective-permute-start | bytes 6291464 | tf_op jit(solution)/shard_map/ppermute | solution.py:22
  34.8 5.1 %copy-start.9 = (s32[32,5]{0,1:T(8,128)S(1)}, s32[32,5]{0,1:T(8,128)}, u32[]{:S(2)}) copy-start(s32[32,5]{0,1:T(8,128)} %param.8) | copy-start | bytes 1924
  34.8 69.9 %all-to-all-start = ((bf16[512,4,1024]{2,0,1:T(8,128)(2,1)}), bf16[512,4,1024]{2,0,1:T(8,128)(2,1)}, u32[]{:S(2)}, u32[]{:S(2)}) async-start(bf16[512,4,1024]{2,0,1:T(8,128)(2,1)} %bitcast.31), calls=%async_computation | async-start | bytes 8388608 | tf_op jit(solution)/shard_map/all_to_all | solution.py:427
  40.3 64.5 %collective-permute-start.1 = (bf16[2048,512]{1,0:T(8,128)(2,1)S(1)}, bf16[2048,512]{1,0:T(8,128)(2,1)}, u32[]{:S(2)}, u32[]{:S(2)}) collective-permute-start(bf16[2048,512]{1,0:T(8,128)(2,1)S(1)} %bitcast.23), channel_id=1, source_target_pairs={{0,1},{2,3},{4,5},{6,7},{8,9},{10,11},{12,13},{14,15},{16,17},{18,... | collective-permute-start | bytes 6291464 | tf_op jit(solution)/shard_map/ppermute | solution.py:422
  43.9 1.1 copy-start.6
  50.3 1.3 copy-start.7
  103.4 6.4 %collective-permute-start.2 = (bf16[2048,512]{1,0:T(8,128)(2,1)}, bf16[2048,512]{1,0:T(8,128)(2,1)}, u32[]{:S(2)}, u32[]{:S(2)}) collective-permute-start(bf16[2048,512]{1,0:T(8,128)(2,1)} %collective-permute-done.two_ref), channel_id=1, source_target_pairs={{1,0},{3,2},{5,4},{7,6},{9,8},{11,10},{13,12},{15,14},{17,16},{19,... | collective-permute-start | bytes 6291464 | tf_op jit(solution)/shard_map/ppermute | solution.py:426
  109.8 1.2 copy-start.4
  138.9 1.3 copy-start.2
  140.2 34.0 %all-to-all-start.2 = ((bf16[4,512,512]{2,1,0:T(8,128)(2,1)}), bf16[4,512,512]{2,1,0:T(8,128)(2,1)S(1)}, u32[]{:S(2)}, u32[]{:S(2)}) async-start(bf16[4,512,512]{2,1,0:T(8,128)(2,1)} %bitcast.29), calls=%async_computation.2 | async-start | bytes 4194304 | tf_op jit(solution)/shard_map/all_to_all | solution.py:444
  143.8 1.2 copy-start.5
  172.9 1.3 copy-start.3
